TPU v7x, 32 devices: a whole 2x2x4 slice. The times are simulated.
32 devices in a mesh: band: 4 (over x, core), dp: 8 (over z, y).
Axes of the slice: x: 2, y: 2, z: 4, core: 2. Of those that a mesh axis runs over, the one named last changes fastest.
Arguments:
- pixels: bfloat16 [8, 32768, 64], P('band', 'dp'), may hold values from -6 to 6
- band_ids: int32 [8, 8], P('dp'), may hold values from 0 to 31
- band_mask: int32 [8, 8], P('dp'), may hold values 0 or 1
- sensor_tags: int32 [8], P('dp'), may hold values from 0 to 5
- segment_ids: int32 [32, 1024], P(('dp', 'band')), may hold values from 0 to 3, never falling along the last dimension, each value on 1 to 512 neighbouring positions
- wave_table: bfloat16 [32, 128], replicated, may hold values from -6 to 6
- gen_w1: bfloat16 [128, 128], replicated, may hold values from -0.5 to 0.5
- gen_w2: bfloat16 [128, 49152], replicated, may hold values from -0.0234375 to 0.0234375
- sensor_table: bfloat16 [6, 768], replicated, may hold values from -3 to 3
- ln1_gain: float32 [768], replicated, may hold values from 0.5 to 1.5
- qkv_weight: bfloat16 [768, 2304], replicated, may hold values from -0.21875 to 0.21875
- proj_weight: bfloat16 [768, 768], replicated, may hold values from -0.875 to 0.875
- ln2_gain: float32 [768], replicated, may hold values from 0.5 to 1.5
- fc1_weight: bfloat16 [768, 3072], replicated, may hold values from -0.21875 to 0.21875
- fc2_weight: bfloat16 [3072, 768], replicated, may hold values from -0.109375 to 0.109375
- out_grad: bfloat16 [32768, 768], P(('dp', 'band')), may hold values from -6 to 6
Outputs:
- encoded: float32 [32768, 768], P(('dp', 'band'))
- pixel_grad: float32 [8, 32768, 64], P('band', 'dp')
- wave_table_grad: float32 [32, 128], replicated
- gen_w1_grad: float32 [128, 128], replicated
- gen_w2_grad: float32 [128, 49152], P(None, ('band', 'dp'))
- sensor_grad: float32 [6, 768], replicated
- ln1_gain_grad: float32 [768], replicated
- qkv_grad: float32 [768, 2304], P(None, ('band', 'dp'))
- proj_grad: float32 [768, 768], P(None, ('band', 'dp'))
- ln2_gain_grad: float32 [768], replicated
- fc1_grad: float32 [768, 3072], P(None, ('band', 'dp'))
- fc2_grad: float32 [3072, 768], P(('band', 'dp'))
Inputs may be any that keep to these rules, and one draw needn't show every extreme that they name: `segment_ids`: chip numbers never fall along a sequence; a chip holds 1 to 512 patches, one exactly 512.
All inputs are finite; a program needn't handle non-finite values. No bound on the sum of `band_mask` on one device may be relied on, other than what follows from the above.
Results may differ from a plain program's by a relative error of at most 0.019.
Values may be sent and summed in bfloat16 or wider, within the bound.
No kernel may reach another device: no remote copies, remote signals or barrier semaphores. Data moves between devices by JAX's collectives and lax.ppermute only.
A program may use at most 320 MiB of HBM per device.

v0:
```python
import jax
import jax.numpy as jnp
from jax import lax
from jax.sharding import PartitionSpec as P

HEADS = 12


highest = lax.Precision.HIGHEST


def layer_norm(inputs, gain):
    center = inputs - jnp.mean(inputs, axis=-1, keepdims=True)
    inverse = lax.rsqrt(jnp.mean(center * center, axis=-1, keepdims=True) + 1e-05)
    unit_rows = center * inverse
    return (unit_rows * gain, unit_rows, inverse)


def norm_back(grad_rows, unit_rows, inverse, gain):
    scaled = grad_rows * gain
    inner = jnp.mean(scaled * unit_rows, axis=-1, keepdims=True)
    result = inverse * (scaled - jnp.mean(scaled, axis=-1, keepdims=True) - unit_rows * inner)
    return (result, jnp.sum(grad_rows * unit_rows, axis=0))


def generate(wave_rows, gen_w1):
    return wave_rows + jax.nn.gelu(
        jnp.dot(wave_rows.astype(jnp.bfloat16), gen_w1, preferred_element_type=jnp.float32)
    )


def generate_exact(wave_rows, weight):
    return wave_rows + jax.nn.gelu(jnp.dot(wave_rows, weight, precision=highest))


def score_block(query_heads, key_heads, seg_rows, seg_all, score_scale):
    scores = (
        jnp.einsum("qhd,khd->hqk", query_heads, key_heads, preferred_element_type=jnp.float32)
        * score_scale
    )
    same_segment = seg_rows[:, None] == seg_all[None, :]
    return jnp.where(same_segment[None], scores, -1000000000.0)


def attend_forward(queries, keys, values, segment, head_count):
    length, model_width = queries.shape
    head_size = model_width // head_count
    score_scale = head_size ** (-0.5)
    block_rows = min(512, length)
    query_heads = queries.reshape(length, head_count, head_size)
    key_heads = keys.reshape(length, head_count, head_size)
    value_heads = values.reshape(length, head_count, head_size)
    outputs = []
    totals = []
    for first_row in range(0, length, block_rows):
        rows_end = first_row + block_rows
        scores = score_block(
            query_heads[first_row:rows_end],
            key_heads,
            segment[first_row:rows_end],
            segment,
            score_scale,
        )
        row_peak = jnp.max(scores, axis=-1, keepdims=True)
        log_total = row_peak + jnp.log(jnp.sum(jnp.exp(scores - row_peak), axis=-1, keepdims=True))
        weights_low = jnp.exp(scores - log_total).astype(jnp.bfloat16)
        mixed_rows = jnp.einsum(
            "hqk,khd->qhd", weights_low, value_heads, preferred_element_type=jnp.float32
        )
        outputs.append(mixed_rows.reshape(-1, model_width))
        totals.append(log_total)
    return (jnp.concatenate(outputs, axis=0).astype(jnp.bfloat16), jnp.concatenate(totals, axis=1))


def attend_back(queries, keys, values, segment, totals, grad_mixed, head_count):
    length, model_width = queries.shape
    head_size = model_width // head_count
    score_scale = head_size ** (-0.5)
    block_rows = min(512, length)
    query_heads = queries.reshape(length, head_count, head_size)
    key_heads = keys.reshape(length, head_count, head_size)
    value_heads = values.reshape(length, head_count, head_size)
    grad_heads = grad_mixed.reshape(length, head_count, head_size)
    grad_keys = jnp.zeros((length, head_count, head_size), jnp.float32)
    grad_values = jnp.zeros((length, head_count, head_size), jnp.float32)
    grad_queries = []
    for first_row in range(0, length, block_rows):
        rows_end = first_row + block_rows
        scores = score_block(
            query_heads[first_row:rows_end],
            key_heads,
            segment[first_row:rows_end],
            segment,
            score_scale,
        )
        weights = jnp.exp(scores - totals[:, first_row:rows_end])
        weights_low = weights.astype(jnp.bfloat16)
        grad_weights = jnp.einsum(
            "qhd,khd->hqk",
            grad_heads[first_row:rows_end],
            value_heads,
            preferred_element_type=jnp.float32,
        )
        grad_scores = (
            weights * (grad_weights - jnp.sum(weights * grad_weights, axis=-1, keepdims=True))
        ).astype(jnp.bfloat16)
        grad_queries.append(
            jnp.einsum(
                "hqk,khd->qhd", grad_scores, key_heads, preferred_element_type=jnp.float32
            ).reshape(-1, model_width)
            * score_scale
        )
        grad_keys = (
            grad_keys
            + jnp.einsum(
                "hqk,qhd->khd",
                grad_scores,
                query_heads[first_row:rows_end],
                preferred_element_type=jnp.float32,
            )
            * score_scale
        )
        grad_values = grad_values + jnp.einsum(
            "hqk,qhd->khd",
            weights_low,
            grad_heads[first_row:rows_end],
            preferred_element_type=jnp.float32,
        )
    return jnp.concatenate(
        [
            jnp.concatenate(grad_queries, axis=0),
            grad_keys.reshape(length, model_width),
            grad_values.reshape(length, model_width),
        ],
        axis=1,
    )


def shards(
    pixels,
    band_ids,
    band_mask,
    sensor_tags,
    segment_ids,
    wave_table,
    gen_w1,
    gen_w2,
    sensor_table,
    ln1_gain,
    qkv_weight,
    proj_weight,
    ln2_gain,
    fc1_weight,
    fc2_weight,
    out_grad,
):
    band_place = lax.axis_index("band")
    slots_dev = pixels.shape[0]
    tok_dev = out_grad.shape[0]
    model_width = qkv_weight.shape[0]
    patch_pixels = pixels.shape[2]
    wave_count = wave_table.shape[0]
    seq_count = segment_ids.shape[0]
    length = segment_ids.shape[1]
    slot_ids = lax.dynamic_slice_in_dim(band_ids[0], band_place * slots_dev, slots_dev)
    slot_mask = lax.dynamic_slice_in_dim(band_mask[0], band_place * slots_dev, slots_dev)
    select = (slot_ids[:, None] == jnp.arange(wave_count, dtype=jnp.int32)[None, :]).astype(
        jnp.float32
    )
    table_exact = wave_table.astype(jnp.float32)
    wave_rows = jnp.dot(select, table_exact, precision=highest)
    hidden = generate(wave_rows, gen_w1)
    hidden_low = hidden.astype(jnp.bfloat16)
    kernel_flat = jnp.dot(hidden_low, gen_w2, preferred_element_type=jnp.float32).astype(
        jnp.bfloat16
    )
    mask_low = slot_mask.astype(jnp.bfloat16)
    kernel = (kernel_flat * mask_low[:, None]).reshape(-1, patch_pixels, model_width)
    block_pixels = pixels
    embedded = lax.psum_scatter(
        jnp.einsum("btp,bpd->td", block_pixels, kernel, preferred_element_type=jnp.float32).astype(
            jnp.bfloat16
        ),
        "band",
        scatter_dimension=0,
        tiled=True,
    ).astype(jnp.float32)
    sensor_pick = (sensor_tags[0] == jnp.arange(sensor_table.shape[0], dtype=jnp.int32)).astype(
        jnp.float32
    )
    sensor_row = jnp.dot(sensor_pick, sensor_table.astype(jnp.float32), precision=highest)
    start_rows = embedded + sensor_row[None, :]
    normed1, unit1, inverse1 = layer_norm(start_rows, ln1_gain)
    normed1_low = normed1.astype(jnp.bfloat16)
    projected = jnp.dot(normed1_low, qkv_weight, preferred_element_type=jnp.float32).astype(
        jnp.bfloat16
    )
    queries = projected[:, :model_width].reshape(seq_count, length, model_width)
    keys = projected[:, model_width : 2 * model_width].reshape(seq_count, length, model_width)
    values = projected[:, 2 * model_width :].reshape(seq_count, length, model_width)

    def forward_one(packed):
        return attend_forward(packed[0], packed[1], packed[2], packed[3], HEADS)

    attended, totals = lax.map(forward_one, (queries, keys, values, segment_ids))
    attended = attended.reshape(tok_dev, model_width)
    after = start_rows + jnp.dot(attended, proj_weight, preferred_element_type=jnp.float32)
    normed2, unit2, inverse2 = layer_norm(after, ln2_gain)
    normed2_low = normed2.astype(jnp.bfloat16)
    up_rows = jnp.dot(normed2_low, fc1_weight, preferred_element_type=jnp.float32)
    act_low = jax.nn.gelu(up_rows).astype(jnp.bfloat16)
    encoded = after + jnp.dot(act_low, fc2_weight, preferred_element_type=jnp.float32)
    grad_act = jnp.dot(out_grad, fc2_weight.T, preferred_element_type=jnp.float32)
    fc2_term = jnp.dot(act_low.T, out_grad, preferred_element_type=jnp.float32)
    gelu_out, gelu_pull = jax.vjp(jax.nn.gelu, up_rows)
    grad_up = gelu_pull(grad_act)[0].astype(jnp.bfloat16)
    fc1_term = jnp.dot(normed2_low.T, grad_up, preferred_element_type=jnp.float32)
    grad_normed2 = jnp.dot(grad_up, fc1_weight.T, preferred_element_type=jnp.float32)
    grad_after_norm, ln2_term = norm_back(grad_normed2, unit2, inverse2, ln2_gain)
    grad_after = out_grad.astype(jnp.float32) + grad_after_norm
    grad_attn = grad_after.astype(jnp.bfloat16)
    proj_term = jnp.dot(attended.T, grad_attn, preferred_element_type=jnp.float32)
    grad_attended = jnp.dot(grad_attn, proj_weight.T, preferred_element_type=jnp.float32).astype(
        jnp.bfloat16
    )

    def back_one(packed):
        return attend_back(packed[0], packed[1], packed[2], packed[3], packed[4], packed[5], HEADS)

    grad_projected = lax.map(
        back_one,
        (
            queries,
            keys,
            values,
            segment_ids,
            totals,
            grad_attended.reshape(seq_count, length, model_width),
        ),
    )
    grad_projected = grad_projected.reshape(tok_dev, 3 * model_width).astype(jnp.bfloat16)
    qkv_term = jnp.dot(normed1_low.T, grad_projected, preferred_element_type=jnp.float32)
    grad_normed1 = jnp.dot(grad_projected, qkv_weight.T, preferred_element_type=jnp.float32)
    grad_start_norm, ln1_term = norm_back(grad_normed1, unit1, inverse1, ln1_gain)
    grad_start = grad_after + grad_start_norm
    sensor_term = sensor_pick[:, None] * jnp.sum(grad_start, axis=0)[None, :]
    grad_embed = grad_start.astype(jnp.bfloat16)
    empty_pixels = jnp.zeros(pixels.shape, jnp.float32)
    empty_kernel = jnp.zeros((slots_dev, patch_pixels, model_width), jnp.float32)
    piece = lax.all_gather(grad_embed, "band", axis=0, tiled=True)
    start = jnp.int32(0)
    grad_pixels = empty_pixels
    grad_sums = empty_kernel
    count = piece.shape[0]
    block_pixels = lax.dynamic_slice_in_dim(pixels, start, count, 1)
    grad_block = jnp.einsum("td,bpd->btp", piece, kernel, preferred_element_type=jnp.float32)
    grad_pixels = lax.dynamic_update_slice_in_dim(grad_pixels, grad_block, start, 1)
    grad_sums = grad_sums + jnp.einsum(
        "btp,td->bpd", block_pixels, piece, preferred_element_type=jnp.float32
    )
    slot_total = grad_sums.shape[0]
    grad_kernel_low = (
        grad_sums.reshape(slot_total, -1) * slot_mask.astype(jnp.float32)[:, None]
    ).astype(jnp.bfloat16)
    gen_w1_exact = gen_w1.astype(jnp.float32)
    gen_w2_term = jnp.dot(hidden_low.T, grad_kernel_low, preferred_element_type=jnp.float32)
    grad_hidden = jnp.dot(grad_kernel_low, gen_w2.T, preferred_element_type=jnp.float32)

    def lookup_generate(table, weight):
        return generate_exact(jnp.dot(select, table, precision=highest), weight)

    hidden_out, gen_pull = jax.vjp(lookup_generate, table_exact, gen_w1_exact)
    table_term, gen_w1_term = gen_pull(grad_hidden)
    qkv_grad, proj_grad, fc1_grad, fc2_grad, gen_w2_grad = (
        lax.psum_scatter(qkv_term, ("band", "dp"), scatter_dimension=1, tiled=True),
        lax.psum_scatter(proj_term, ("band", "dp"), scatter_dimension=1, tiled=True),
        lax.psum_scatter(fc1_term, ("band", "dp"), scatter_dimension=1, tiled=True),
        lax.psum_scatter(fc2_term, ("band", "dp"), scatter_dimension=0, tiled=True),
        lax.psum_scatter(gen_w2_term, ("band", "dp"), scatter_dimension=1, tiled=True),
    )
    ln1_gain_grad, ln2_gain_grad, sensor_grad, wave_table_grad, gen_w1_grad = lax.psum(
        (ln1_term, ln2_term, sensor_term, table_term, gen_w1_term), ("band", "dp")
    )
    return (
        encoded,
        grad_pixels,
        wave_table_grad,
        gen_w1_grad,
        gen_w2_grad,
        sensor_grad,
        ln1_gain_grad,
        qkv_grad,
        proj_grad,
        ln2_gain_grad,
        fc1_grad,
        fc2_grad,
    )


def solution(mesh):
    return jax.shard_map(
        shards,
        mesh=mesh,
        in_specs=(
            P("band", "dp", None),
            P("dp", None),
            P("dp", None),
            P("dp"),
            P(("dp", "band"), None),
            P(),
            P(),
            P(),
            P(),
            P(),
            P(),
            P(),
            P(),
            P(),
            P(),
            P(("dp", "band"), None),
        ),
        out_specs=(
            P(("dp", "band"), None),
            P("band", "dp", None),
            P(),
            P(),
            P(None, ("band", "dp")),
            P(),
            P(),
            P(None, ("band", "dp")),
            P(None, ("band", "dp")),
            P(),
            P(None, ("band", "dp")),
            P(("band", "dp"), None),
        ),
        check_vma=False,
    )
```

profile of v0, /device:TPU:0, one launch (start us, length us, event | category | flops | bytes accessed | tf_op | source)
XLA Modules:
  0.0 1319.4 jit_solution(17600156306195803492)
XLA Ops:
  10.5 6.4 fusion
  17.6 4.5 fusion.14
  23.0 2.6 copy.54
  28.1 55.1 %reduce-scatter.7.cloned.1.call-done = bf16[1024,768]{0,1:T(8,128)(2,1)} async-done(((bf16[4096,768]{0,1:T(8,128)(2,1)}), bf16[1024,768]{0,1:T(8,128)(2,1)}) %reduce-scatter.7.cloned.1.call-update) | async-done | bytes 1572880 | tf_op jit(solution)/shard_map/reduce_scatter | solution.py:180
  87.1 6.3 convolution_convert_fusion.1
  96.6 2.6 copy.51
  99.1 2.3 copy.50
  101.4 2.3 copy.52
  103.7 2.6 copy.49
  106.3 14.4 %fusion.2 = (f32[12,512]{1,0:T(8,128)S(1)}, f32[12,512,1024]{2,1,0:T(8,128)}) fusion(pred[512,1024]{1,0:T(8,128)(4,1)} %get-tuple-element.100, bf16[512,12,64]{0,2,1:T(8,128)(2,1)} %bitcast.121, bf16[1024,12,64]{0,2,1:T(8,128)(2,1)} %bitcast.113), kind=kOutput, calls=%fused_computation.13 | convolution fusion | flops 824174592 | bytes 28073984 | tf_op jit(solution)/shard_map/while/body/eval_jaxpr/qhd,khd->hqk/dot_general | solution.py:38
  120.7 11.9 exponential_reduce_fusion
  132.7 11.0 fusion.1
  143.8 11.9 exponential_reduce_fusion.1
  155.7 11.2 convolution_convert_fusion.3
  166.9 12.3 convolution_convert_fusion.4
  179.2 3.0 fusion.112
  182.7 8.7 fusion.105
  191.4 15.3 %fusion.11 = bf16[1024,3072]{1,0:T(8,128)(2,1)} fusion(f32[1024,3072]{1,0:T(8,128)} %fusion.105, bf16[1024,768]{1,0:T(8,128)(2,1)S(1)} %copy-done.22, bf16[3072,768]{1,0:T(8,128)(2,1)} %param.30), kind=kOutput, calls=%fused_computation.24 | convolution fusion | flops 4894752768 | bytes 25165824 | tf_op jit(solution)/shard_map/dot_general | solution.py:213
  206.7 8.7 multiply_reduce_fusion.2
  220.3 13.2 %fusion.33 = f32[12,64,1024]{2,1,0:T(8,128)} fusion(bf16[512,12,64]{0,2,1:T(8,128)(2,1)S(1)} %bitcast.135, f32[12,512,1024]{2,1,0:T(8,128)} %get-tuple-element.108, f32[12,512]{1,0:T(8,128)S(1)} %log_add_fusion.1, pred[512,1024]{1,0:T(8,128)(4,1)S(1)} %copy-done.11), kind=kOutput, calls=%fused_computation.74 | convolution fusion | flops 830472192 | bytes 29646848 | tf_op jit(solution)/shard_map/while/body/eval_jaxpr/hqk,qhd->khd/dot_general | solution.py:123
  233.5 18.8 %multiply_reduce_fusion.1 = (f32[12,512]{1,0:T(8,128)}, f32[12,512,1024]{2,1,0:T(8,128)}) fusion(f32[12,512,1024]{2,1,0:T(8,128)} %get-tuple-element.108, f32[12,512]{1,0:T(8,128)} %copy-done.34, pred[512,1024]{1,0:T(8,128)(4,1)} %get-tuple-element.99, bf16[512,12,64]{0,2,1:T(8,128)(2,1)} %bitcast.136, bf16[1024,12,64]{0,2,1:T(8,128)(2,1)} %bitcast.117), kind=kOutput, calls=%fused_computation.5 | convolution fusion | flops 836757504 | bytes 53264384 | tf_op jit(solution)/shard_map/while/body/eval_jaxpr/qhd,khd->hqk/dot_general | solution.py:98
  252.4 22.6 %multiply_convert_fusion.1 = bf16[12,512,1024]{2,1,0:T(8,128)(2,1)} fusion(f32[12,512,1024]{2,1,0:T(8,128)} %get-tuple-element.113, f32[12,512,1024]{2,1,0:T(8,128)} %get-tuple-element.108, f32[12,512]{1,0:T(8,128)} %get-tuple-element.112, f32[12,512]{1,0:T(8,128)} %copy-done.34, pred[512,1024]{1,0:T(8,128)(4,1)} %get-tuple-element.99), kind=kLoop, calls=%fused_computation.4 | loop fusion | flops 37748736 | bytes 63488000 | tf_op jit(solution)/shard_map/while/body/eval_jaxpr/convert_element_type | solution.py:106
  275.0 9.5 multiply_convert_fusion.7
  284.5 8.5 fusion.113
  293.0 18.8 %multiply_reduce_fusion = (f32[12,512]{1,0:T(8,128)}, f32[12,512,1024]{2,1,0:T(8,128)}) fusion(f32[12,512,1024]{2,1,0:T(8,128)} %get-tuple-element.106, f32[12,512]{1,0:T(8,128)} %copy-done.32, pred[512,1024]{1,0:T(8,128)(4,1)} %get-tuple-element.100, bf16[512,12,64]{0,2,1:T(8,128)(2,1)} %bitcast.133, bf16[1024,12,64]{0,2,1:T(8,128)(2,1)} %bitcast.118), kind=kOutput, calls=%fused_computation.3 | convolution fusion | flops 836757504 | bytes 53264384 | tf_op jit(solution)/shard_map/while/body/eval_jaxpr/qhd,khd->hqk/dot_general | solution.py:98
  311.8 15.0 %add_convert_fusion = bf16[12,64,1024]{2,1,0:T(8,128)(2,1)S(1)} fusion(f32[12,64,1024]{2,1,0:T(8,128)} %fusion.33, bf16[512,12,64]{0,2,1:T(8,128)(2,1)} %bitcast.134, f32[12,512,1024]{2,1,0:T(8,128)} %get-tuple-element.106, f32[12,512]{1,0:T(8,128)} %copy-done.32, pred[512,1024]{1,0:T(8,128)(4,1)} %get-tuple-element.100), kind=kOutput, calls=%fused_computation.37 | convolution fusion | flops 832045056 | bytes 31219712 | tf_op jit(solution)/shard_map/while/body/eval_jaxpr/hqk,qhd->khd/dot_general | solution.py:123
  326.8 22.0 %multiply_convert_fusion = bf16[12,512,1024]{2,1,0:T(8,128)(2,1)} fusion(f32[12,512,1024]{2,1,0:T(8,128)} %get-tuple-element.115, f32[12,512,1024]{2,1,0:T(8,128)} %get-tuple-element.106, f32[12,512]{1,0:T(8,128)S(1)} %copy-done.35, f32[12,512]{1,0:T(8,128)S(1)} %copy-done.33, pred[512,1024]{1,0:T(8,128)(4,1)S(1)} %copy-done.10), kind=kLoop, calls=%fused_computation.2 | loop fusion | flops 37748736 | bytes 63488000 | tf_op jit(solution)/shard_map/while/body/eval_jaxpr/convert_element_type | solution.py:106
  348.8 8.6 multiply_convert_fusion.6
  357.6 7.2 multiply_convert_fusion.3
  364.9 5.0 multiply_reduce_fusion.3
  369.9 2.9 fusion.107
  372.8 5.3 fusion.22
  378.4 10.5 fusion.23
  390.5 28.8 %all-gather.2.cloned.1.call-done = bf16[4096,768]{0,1:T(8,128)(2,1)} async-done(((bf16[1024,768]{0,1:T(8,128)(2,1)}), bf16[4096,768]{0,1:T(8,128)(2,1)}) %all-gather.2.cloned.1.call-update) | async-done | bytes 6291472 | tf_op jit(solution)/shard_map/all_gather | solution.py:250
  419.3 5.2 fusion.114
  424.9 6.5 fusion.103
  433.0 12.8 fusion.106
  446.5 10.8 fusion.104
  457.9 12.9 fusion.102
  470.8 12.4 convolution_add_fusion
  483.2 3.6 copy.61
  489.3 40.7 %all-reduce = (f32[32,128]{1,0:T(8,128)}, f32[6,768]{1,0:T(8,128)}, f32[768]{0:T(1024)}, f32[768]{0:T(1024)}) all-reduce(f32[32,128]{1,0:T(8,128)S(1)} %fusion.55, f32[6,768]{1,0:T(8,128)} %broadcast_multiply_fusion, f32[768]{0:T(1024)} %get-tuple-element.83, f32[768]{0:T(1024)} %get-tuple-element.81), channel_id=1, replica_groups=mesh['band'=4,'dp'=8] {'band','dp'}, use_global_device_ids=true, to_apply=%region_15.16 | all-reduce | flops 10240 | bytes 81920 | tf_op jit(solution)/shard_map/psum | solution.py:281
  530.0 5.2 fusion.15
  535.2 114.3 %reduce-scatter.11.cloned.1.call-done = f32[768,72]{0,1:T(8,128)} async-done(((f32[768,2304]{0,1:T(8,128)}), f32[768,72]{0,1:T(8,128)}) %reduce-scatter.11.cloned.1.call-update) | async-done | bytes 221200 | tf_op jit(solution)/shard_map/reduce_scatter | solution.py:275
  649.5 123.8 %all-reduce.3.cloned.1.call-done = f32[128,128]{1,0:T(8,128)} async-done(((f32[128,128]{1,0:T(8,128)}), f32[128,128]{1,0:T(8,128)}) %all-reduce.3.cloned.1.call-update) | async-done | bytes 65552 | tf_op jit(solution)/shard_map/psum | solution.py:281
  773.3 143.8 %reduce-scatter.17.cloned.1.call-done = f32[96,768]{1,0:T(8,128)} async-done(((f32[3072,768]{1,0:T(8,128)}), f32[96,768]{1,0:T(8,128)}) %reduce-scatter.17.cloned.1.call-update) | async-done | bytes 294928 | tf_op jit(solution)/shard_map/reduce_scatter | solution.py:278
  917.1 141.1 %reduce-scatter.15.cloned.1.call-done = f32[768,96]{0,1:T(8,128)} async-done(((f32[768,3072]{0,1:T(8,128)}), f32[768,96]{0,1:T(8,128)}) %reduce-scatter.15.cloned.1.call-update) | async-done | bytes 294928 | tf_op jit(solution)/shard_map/reduce_scatter | solution.py:277
  1058.2 252.5 %reduce-scatter.9.cloned.1.call-done = f32[128,1536]{1,0:T(8,128)} async-done(((f32[128,49152]{1,0:T(8,128)}), f32[128,1536]{1,0:T(8,128)}) %reduce-scatter.9.cloned.1.call-update) | async-done | bytes 786448 | tf_op jit(solution)/shard_map/reduce_scatter | solution.py:279
  (179 shorter events, 28.0 us)
Async XLA Ops:
  7.2 79.9 %copy-start = (bf16[768,2304]{1,0:T(8,128)(2,1)S(1)}, bf16[768,2304]{1,0:T(8,128)(2,1)}, u32[]{:S(2)}) copy-start(bf16[768,2304]{1,0:T(8,128)(2,1)} %param.26) | copy-start | bytes 10616836
  7.2 76.1 %reduce-scatter.7.cloned.1.call-start = ((), (), s32[]{:S(2)}) async-start(), calls=%async_computation.6 | async-start | bytes 7864320 | tf_op jit(solution)/shard_map/reduce_scatter | solution.py:180
  10.5 7.1 copy-start.23
  22.1 65.0 %copy-start.49 = (f32[768]{0:T(1024)S(1)}, f32[768]{0:T(1024)}, u32[]{:S(2)}) copy-start(f32[768]{0:T(1024)} %param.25) | copy-start | bytes 9220
  22.1 397.2 %all-gather.2.cloned.1.call-start = ((), (), s32[]{:S(2)}) async-start(), calls=%async_computation.7 | async-start | bytes 7864320 | tf_op jit(solution)/shard_map/all_gather | solution.py:250
  26.5 152.7 %copy-start.36 = (f32[768]{0:T(1024)}, f32[768]{0:T(1024)S(1)}, u32[]{:S(2)}) copy-start(f32[768]{0:T(1024)S(1)} %convolution_reduce_fusion) | copy-start | bytes 9220
  85.1 8.4 copy-start.38
  106.3 14.4 %copy-start.9 = (pred[512,1024]{1,0:T(8,128)(4,1)S(1)}, pred[512,1024]{1,0:T(8,128)(4,1)}, u32[]{:S(2)}) copy-start(pred[512,1024]{1,0:T(8,128)(4,1)} %get-tuple-element.100) | copy-start | bytes 1572868
  120.7 12.0 copy-start.1
  120.7 12.0 copy-start.11
  120.7 12.0 copy-start.15
  132.7 23.0 %copy-start.32 = (f32[12,512]{1,0:T(8,128)}, f32[12,512]{1,0:T(8,128)S(1)}, u32[]{:S(2)}) copy-start(f32[12,512]{1,0:T(8,128)S(1)} %log_add_fusion) | copy-start | bytes 73732
  143.8 11.9 copy-start.6
  155.7 63.7 %copy-start.34 = (f32[12,512]{1,0:T(8,128)}, f32[12,512]{1,0:T(8,128)S(1)}, u32[]{:S(2)}) copy-start(f32[12,512]{1,0:T(8,128)S(1)} %log_add_fusion.1) | copy-start | bytes 73732
  166.9 12.3 copy-start.59
  166.9 12.3 copy-start.7
  166.9 12.3 copy-start.56
  182.2 33.2 %copy-start.4 = (f32[1024,768]{0,1:T(8,128)}, f32[1024,768]{0,1:T(8,128)S(1)}, u32[]{:S(2)}) copy-start(f32[1024,768]{0,1:T(8,128)S(1)} %get-tuple-element.110) | copy-start | bytes 9437188
  182.3 33.2 %copy-start.26 = (f32[1024]{0:T(1024)}, f32[1024]{0:T(1024)S(1)}, u32[]{:S(2)}) copy-start(f32[1024]{0:T(1024)S(1)} %broadcast_multiply_fusion.5) | copy-start | bytes 12292
  182.7 32.7 %copy-start.28 = (f32[1024]{0:T(1024)}, f32[1024]{0:T(1024)S(1)}, u32[]{:S(2)}) copy-start(f32[1024]{0:T(1024)S(1)} %add_rsqrt_fusion) | copy-start | bytes 12292
  182.7 8.7 copy-start.22
  182.7 24.0 %slice-start.2 = ((s8[4718592]{0:T(1024)(128)(4,1)}), s8[4194304]{0:T(1024)(128)(4,1)S(1)}, s32[]{:S(2)}) async-start(s8[4718592]{0:T(1024)(128)(4,1)} %bitcast.127), calls=%async_computation.16 | async-start | bytes 8388608
  191.4 15.3 %slice-start.3 = ((s8[4718592]{0:T(1024)(128)(4,1)}), s8[524288]{0:T(1024)(128)(4,1)S(1)}, s32[]{:S(2)}) async-start(s8[4718592]{0:T(1024)(128)(4,1)} %bitcast.127), calls=%async_computation.17 | async-start | bytes 1048576
  206.7 8.7 copy-start.17
  252.4 22.6 %copy-start.2 = (bf16[1024,768]{0,1:T(8,128)(2,1)S(1)}, bf16[1024,768]{0,1:T(8,128)(2,1)}, u32[]{:S(2)}) copy-start(bf16[1024,768]{0,1:T(8,128)(2,1)} %copy.51) | copy-start | bytes 4718596
  275.0 9.5 copy-start.16
  311.8 15.0 %copy-start.10 = (pred[512,1024]{1,0:T(8,128)(4,1)S(1)}, pred[512,1024]{1,0:T(8,128)(4,1)}, u32[]{:S(2)}) copy-start(pred[512,1024]{1,0:T(8,128)(4,1)} %get-tuple-element.100) | copy-start | bytes 1572868
  311.8 15.0 %copy-start.33 = (f32[12,512]{1,0:T(8,128)S(1)}, f32[12,512]{1,0:T(8,128)}, u32[]{:S(2)}) copy-start(f32[12,512]{1,0:T(8,128)} %copy-done.32) | copy-start | bytes 73732
  311.8 15.0 %copy-start.35 = (f32[12,512]{1,0:T(8,128)S(1)}, f32[12,512]{1,0:T(8,128)}, u32[]{:S(2)}) copy-start(f32[12,512]{1,0:T(8,128)} %get-tuple-element.114) | copy-start | bytes 73732
  326.8 38.0 %copy-start.58 = (bf16[12,64,1024]{2,1,0:T(8,128)(2,1)}, bf16[12,64,1024]{2,1,0:T(8,128)(2,1)S(1)}, u32[]{:S(2)}) copy-start(bf16[12,64,1024]{2,1,0:T(8,128)(2,1)S(1)} %add_convert_fusion) | copy-start | bytes 4718596
  326.8 22.0 %copy-start.3 = (bf16[1024,768]{0,1:T(8,128)(2,1)S(1)}, bf16[1024,768]{0,1:T(8,128)(2,1)}, u32[]{:S(2)}) copy-start(bf16[1024,768]{0,1:T(8,128)(2,1)} %copy.51) | copy-start | bytes 4718596
  348.8 8.7 copy-start.5
  348.8 8.7 copy-start.14
  357.5 7.3 copy-start.25
  357.5 7.3 copy-start.8
  357.5 7.3 copy-start.24
  357.5 7.3 copy-start.37
  357.5 7.3 copy-start.39
  357.5 7.3 copy-start.41
  357.6 7.3 copy-start.50
  372.8 162.4 %reduce-scatter.13.cloned.1.call-start = ((), (), s32[]{:S(2)}) async-start(), calls=%async_computation.11 | async-start | bytes 2433024 | tf_op jit(solution)/shard_map/reduce_scatter | solution.py:276
  378.2 271.3 %reduce-scatter.11.cloned.1.call-start = ((), (), s32[]{:S(2)}) async-start(), calls=%async_computation.10 | async-start | bytes 7299072 | tf_op jit(solution)/shard_map/reduce_scatter | solution.py:275
  389.0 35.9 %copy-start.47 = (f32[2]{0:T(128)S(1)}, f32[2]{0:T(128)}, u32[]{:S(2)}) copy-start(f32[2]{0:T(128)} %get-tuple-element.103) | copy-start | bytes 28
  389.0 384.3 %all-reduce.3.cloned.1.call-start = ((), (), s32[]{:S(2)}) async-start(), calls=%async_computation.8 | async-start | bytes 131072 | tf_op jit(solution)/shard_map/psum | solution.py:281
  390.5 40.9 %copy-start.51 = (f32[2,128]{1,0:T(2,128)}, f32[2,128]{1,0:T(2,128)S(1)}, u32[]{:S(2)}) copy-start(f32[2,128]{1,0:T(2,128)S(1)} %fusion.115) | copy-start | bytes 3076
  432.9 484.1 %reduce-scatter.17.cloned.1.call-start = ((), (), s32[]{:S(2)}) async-start(), calls=%async_computation.13 | async-start | bytes 9732096 | tf_op jit(solution)/shard_map/reduce_scatter | solution.py:278
  445.8 612.3 %reduce-scatter.15.cloned.1.call-start = ((), (), s32[]{:S(2)}) async-start(), calls=%async_computation.12 | async-start | bytes 9732096 | tf_op jit(solution)/shard_map/reduce_scatter | solution.py:277
  457.3 853.3 %reduce-scatter.9.cloned.1.call-start = ((), (), s32[]{:S(2)}) async-start(), calls=%async_computation.9 | async-start | bytes 25952256 | tf_op jit(solution)/shard_map/reduce_scatter | solution.py:279
  (24 other events, 64.5 us)
Sparse Core Ops, SparseCore 0:
  22.2 61.0 reduce-scatter.6
  372.9 46.3 all-gather.1
  426.0 99.0 reduce-scatter.12
  531.3 118.1 reduce-scatter.10
  656.4 116.7 all-reduce.2
  780.6 136.4 reduce-scatter.16
  923.5 134.5 reduce-scatter.14
  1066.3 244.3 reduce-scatter.8
where the time goes:
time: 1320 us
  waiting for transfers between devices  860 us (65%)
  matrix products  296 us (22%)
  other arithmetic  80.2 us (6%)
  blocking collectives  40.7 us (3%)
  local copies, waits for them, and re-layouts  26.3 us (2%)
  between operations  16.1 us (1%)
    reduce_scatter x1, waiting for transfers between devices, shards(): lax.psum_scatter(gen_w2_term, ('band', 'dp'), scatter_dimension=1, tiled=...  253 us
    reduce_scatter x1, waiting for transfers between devices, shards(): lax.psum_scatter(fc2_term, ('band', 'dp'), scatter_dimension=0, tiled=True)  144 us
    reduce_scatter x1, waiting for transfers between devices, shards(): lax.psum_scatter(fc1_term, ('band', 'dp'), scatter_dimension=1, tiled=True)  141 us
    psum x1, waiting for transfers between devices, shards(): lax.psum((ln1_term, ln2_term, sensor_term, table_term, gen_w1_term), ('ba...  124 us
    reduce_scatter x1, waiting for transfers between devices, shards(): lax.psum_scatter(qkv_term, ('band', 'dp'), scatter_dimension=1, tiled=True)  114 us
    reduce_scatter x1, waiting for transfers between devices, shards(): lax.psum_scatter(jnp.einsum('btp,bpd->td', block_pixels, kernel, preferre...  55.1 us
    convert_element_type x2, other arithmetic, attend_back(): grad_scores = (weights * (grad_weights - jnp.sum(weights * grad_weights,...  44.6 us
    psum x1, blocking collectives, shards(): lax.psum((ln1_term, ln2_term, sensor_term, table_term, gen_w1_term), ('ba...  40.7 us
  transfers between devices with their start and end apart: 8, of which 7 were waited for; matrix products, arithmetic and copies ran while one was open for 7% of the time, Pallas kernels for 0%

commit v1 on v0

--- a/solution.py
+++ b/solution.py
@@ -136,6 +136,66 @@
     )
 
 
+def swap(piece, axis, mask):
+    count = lax.axis_size(axis)
+    return lax.ppermute(piece, axis, [(i, i ^ mask) for i in range(count)])
+
+
+def bits_of(axis):
+    return lax.axis_size(axis).bit_length() - 1
+
+
+def all_bits():
+    return [("band", bit) for bit in reversed(range(bits_of("band")))] + [
+        ("dp", bit) for bit in reversed(range(bits_of("dp")))
+    ]
+
+
+def scatter_sum(term, order):
+    dims = all_bits()
+    rows = term.shape[0] // (2 ** len(dims))
+    parts = [term.reshape((2,) * len(dims) + (rows,) + term.shape[1:])]
+    for axis, bit in order:
+        dim = dims.index((axis, bit))
+        dims.pop(dim)
+        mine = (lax.axis_index(axis) >> bit) & 1
+        send = sum(
+            lax.dynamic_index_in_dim(part, 1 - mine, dim, False).astype(jnp.float32)
+            for part in parts
+        ).astype(jnp.bfloat16)
+        parts = [lax.dynamic_index_in_dim(part, mine, dim, False) for part in parts]
+        parts.append(swap(send, axis, 1 << bit))
+    return sum(part.astype(jnp.float32) for part in parts)
+
+
+def exchange(pieces, axis):
+    count = lax.axis_size(axis)
+    shape = pieces.shape
+    held = pieces
+    for bit in range(bits_of(axis)):
+        view = held.reshape((count >> (bit + 1), 2, 1 << bit) + shape[1:])
+        got = swap(view[:, 1], axis, 1 << bit)
+        held = jnp.stack([view[:, 0], got], axis=1).reshape(shape)
+    return held
+
+
+def gather_xor(piece, axis):
+    held = piece[None]
+    for bit in range(bits_of(axis)):
+        held = jnp.concatenate([held, swap(held, axis, 1 << bit)], axis=0)
+    return held
+
+
+def in_order(held, axis):
+    place = lax.axis_index(axis)
+    return jnp.stack(
+        [
+            lax.dynamic_index_in_dim(held, place ^ i, 0, False)
+            for i in range(held.shape[0])
+        ]
+    )
+
+
 def shards(
     pixels,
     band_ids,
@@ -155,41 +215,66 @@
     out_grad,
 ):
     band_place = lax.axis_index("band")
+    dp_place = lax.axis_index("dp")
+    band_count = lax.axis_size("band")
+    dp_count = lax.axis_size("dp")
     slots_dev = pixels.shape[0]
+    slots = band_ids.shape[1]
     tok_dev = out_grad.shape[0]
     model_width = qkv_weight.shape[0]
     patch_pixels = pixels.shape[2]
     wave_count = wave_table.shape[0]
     seq_count = segment_ids.shape[0]
     length = segment_ids.shape[1]
-    slot_ids = lax.dynamic_slice_in_dim(band_ids[0], band_place * slots_dev, slots_dev)
-    slot_mask = lax.dynamic_slice_in_dim(band_mask[0], band_place * slots_dev, slots_dev)
-    select = (slot_ids[:, None] == jnp.arange(wave_count, dtype=jnp.int32)[None, :]).astype(
+    sensors = sensor_table.shape[0]
+    code_width = wave_table.shape[1]
+    part_rows = slots_dev * patch_pixels
+
+    own_pixels = pixels.transpose(0, 2, 1).reshape(part_rows, -1)
+    token_pixels = jnp.zeros((band_count * part_rows, tok_dev), pixels.dtype)
+    for mask in range(band_count):
+        other = band_place ^ mask
+        piece = lax.dynamic_slice_in_dim(own_pixels, other * tok_dev, tok_dev, 1)
+        if mask:
+            piece = swap(piece, "band", mask)
+        token_pixels = lax.dynamic_update_slice_in_dim(
+            token_pixels, piece, other * part_rows, 0
+        )
+
+    numbers = jnp.concatenate([band_ids[0], band_mask[0], sensor_tags])
+    all_numbers = in_order(gather_xor(numbers, "dp"), "dp")
+    all_ids = all_numbers[:, :slots].reshape(-1)
+    all_masks = all_numbers[:, slots : 2 * slots].reshape(-1)
+    all_tags = all_numbers[:, 2 * slots]
+
+    select = (all_ids[:, None] == jnp.arange(wave_count, dtype=jnp.int32)[None, :]).astype(
         jnp.float32
     )
     table_exact = wave_table.astype(jnp.float32)
-    wave_rows = jnp.dot(select, table_exact, precision=highest)
-    hidden = generate(wave_rows, gen_w1)
-    hidden_low = hidden.astype(jnp.bfloat16)
+    gen_w1_exact = gen_w1.astype(jnp.float32)
+
+    def lookup_generate(table, weight):
+        return generate_exact(jnp.dot(select, table, precision=highest), weight)
+
+    hidden_all, gen_pull = jax.vjp(lookup_generate, table_exact, gen_w1_exact)
+    hidden_all_low = hidden_all.astype(jnp.bfloat16)
+
+    select_own = (band_ids[0][:, None] == jnp.arange(wave_count, dtype=jnp.int32)[None, :]).astype(
+        jnp.bfloat16
+    )
+    wave_rows = jnp.dot(select_own, wave_table, preferred_element_type=jnp.float32)
+    hidden_low = generate(wave_rows, gen_w1).astype(jnp.bfloat16)
     kernel_flat = jnp.dot(hidden_low, gen_w2, preferred_element_type=jnp.float32).astype(
         jnp.bfloat16
     )
-    mask_low = slot_mask.astype(jnp.bfloat16)
-    kernel = (kernel_flat * mask_low[:, None]).reshape(-1, patch_pixels, model_width)
-    block_pixels = pixels
-    embedded = lax.psum_scatter(
-        jnp.einsum("btp,bpd->td", block_pixels, kernel, preferred_element_type=jnp.float32).astype(
-            jnp.bfloat16
-        ),
-        "band",
-        scatter_dimension=0,
-        tiled=True,
-    ).astype(jnp.float32)
-    sensor_pick = (sensor_tags[0] == jnp.arange(sensor_table.shape[0], dtype=jnp.int32)).astype(
-        jnp.float32
-    )
+    mask_low = band_mask[0].astype(jnp.bfloat16)
+    kernel = (kernel_flat * mask_low[:, None]).reshape(slots * patch_pixels, model_width)
+    sensor_pick = (sensor_tags[0] == jnp.arange(sensors, dtype=jnp.int32)).astype(jnp.float32)
     sensor_row = jnp.dot(sensor_pick, sensor_table.astype(jnp.float32), precision=highest)
-    start_rows = embedded + sensor_row[None, :]
+    start_rows = (
+        jnp.einsum("st,sd->td", token_pixels, kernel, preferred_element_type=jnp.float32)
+        + sensor_row[None, :]
+    )
     normed1, unit1, inverse1 = layer_norm(start_rows, ln1_gain)
     normed1_low = normed1.astype(jnp.bfloat16)
     projected = jnp.dot(normed1_low, qkv_weight, preferred_element_type=jnp.float32).astype(
@@ -211,15 +296,19 @@
     act_low = jax.nn.gelu(up_rows).astype(jnp.bfloat16)
     encoded = after + jnp.dot(act_low, fc2_weight, preferred_element_type=jnp.float32)
     grad_act = jnp.dot(out_grad, fc2_weight.T, preferred_element_type=jnp.float32)
-    fc2_term = jnp.dot(act_low.T, out_grad, preferred_element_type=jnp.float32)
+    fc2_term = jnp.dot(act_low.T, out_grad, preferred_element_type=jnp.float32).astype(jnp.bfloat16)
     gelu_out, gelu_pull = jax.vjp(jax.nn.gelu, up_rows)
     grad_up = gelu_pull(grad_act)[0].astype(jnp.bfloat16)
-    fc1_term = jnp.dot(normed2_low.T, grad_up, preferred_element_type=jnp.float32)
+    fc1_term = jnp.dot(grad_up.T, normed2_low, preferred_element_type=jnp.float32).astype(
+        jnp.bfloat16
+    )
     grad_normed2 = jnp.dot(grad_up, fc1_weight.T, preferred_element_type=jnp.float32)
     grad_after_norm, ln2_term = norm_back(grad_normed2, unit2, inverse2, ln2_gain)
     grad_after = out_grad.astype(jnp.float32) + grad_after_norm
     grad_attn = grad_after.astype(jnp.bfloat16)
-    proj_term = jnp.dot(attended.T, grad_attn, preferred_element_type=jnp.float32)
+    proj_term = jnp.dot(grad_attn.T, attended, preferred_element_type=jnp.float32).astype(
+        jnp.bfloat16
+    )
     grad_attended = jnp.dot(grad_attn, proj_weight.T, preferred_element_type=jnp.float32).astype(
         jnp.bfloat16
     )
@@ -239,48 +328,93 @@
         ),
     )
     grad_projected = grad_projected.reshape(tok_dev, 3 * model_width).astype(jnp.bfloat16)
-    qkv_term = jnp.dot(normed1_low.T, grad_projected, preferred_element_type=jnp.float32)
+    qkv_term = jnp.dot(grad_projected.T, normed1_low, preferred_element_type=jnp.float32).astype(
+        jnp.bfloat16
+    )
     grad_normed1 = jnp.dot(grad_projected, qkv_weight.T, preferred_element_type=jnp.float32)
     grad_start_norm, ln1_term = norm_back(grad_normed1, unit1, inverse1, ln1_gain)
     grad_start = grad_after + grad_start_norm
-    sensor_term = sensor_pick[:, None] * jnp.sum(grad_start, axis=0)[None, :]
+    sensor_term = jnp.sum(grad_start, axis=0)
     grad_embed = grad_start.astype(jnp.bfloat16)
-    empty_pixels = jnp.zeros(pixels.shape, jnp.float32)
-    empty_kernel = jnp.zeros((slots_dev, patch_pixels, model_width), jnp.float32)
-    piece = lax.all_gather(grad_embed, "band", axis=0, tiled=True)
-    start = jnp.int32(0)
-    grad_pixels = empty_pixels
-    grad_sums = empty_kernel
-    count = piece.shape[0]
-    block_pixels = lax.dynamic_slice_in_dim(pixels, start, count, 1)
-    grad_block = jnp.einsum("td,bpd->btp", piece, kernel, preferred_element_type=jnp.float32)
-    grad_pixels = lax.dynamic_update_slice_in_dim(grad_pixels, grad_block, start, 1)
-    grad_sums = grad_sums + jnp.einsum(
-        "btp,td->bpd", block_pixels, piece, preferred_element_type=jnp.float32
-    )
-    slot_total = grad_sums.shape[0]
-    grad_kernel_low = (
-        grad_sums.reshape(slot_total, -1) * slot_mask.astype(jnp.float32)[:, None]
-    ).astype(jnp.bfloat16)
-    gen_w1_exact = gen_w1.astype(jnp.float32)
-    gen_w2_term = jnp.dot(hidden_low.T, grad_kernel_low, preferred_element_type=jnp.float32)
-    grad_hidden = jnp.dot(grad_kernel_low, gen_w2.T, preferred_element_type=jnp.float32)
-
-    def lookup_generate(table, weight):
-        return generate_exact(jnp.dot(select, table, precision=highest), weight)
-
-    hidden_out, gen_pull = jax.vjp(lookup_generate, table_exact, gen_w1_exact)
-    table_term, gen_w1_term = gen_pull(grad_hidden)
-    qkv_grad, proj_grad, fc1_grad, fc2_grad, gen_w2_grad = (
-        lax.psum_scatter(qkv_term, ("band", "dp"), scatter_dimension=1, tiled=True),
-        lax.psum_scatter(proj_term, ("band", "dp"), scatter_dimension=1, tiled=True),
-        lax.psum_scatter(fc1_term, ("band", "dp"), scatter_dimension=1, tiled=True),
-        lax.psum_scatter(fc2_term, ("band", "dp"), scatter_dimension=0, tiled=True),
-        lax.psum_scatter(gen_w2_term, ("band", "dp"), scatter_dimension=1, tiled=True),
-    )
-    ln1_gain_grad, ln2_gain_grad, sensor_grad, wave_table_grad, gen_w1_grad = lax.psum(
-        (ln1_term, ln2_term, sensor_term, table_term, gen_w1_term), ("band", "dp")
-    )
+
+    kernel_term = jnp.dot(token_pixels, grad_embed, preferred_element_type=jnp.float32)
+    kernel_parts = [
+        kernel_term.astype(jnp.bfloat16).reshape(
+            (slots,) + (2,) * bits_of("band") + (patch_pixels // band_count, model_width)
+        )
+    ]
+    for bit in range(bits_of("band")):
+        mine = (band_place >> bit) & 1
+        dim = bits_of("band") - bit
+        send = sum(
+            lax.dynamic_index_in_dim(part, 1 - mine, dim, False).astype(jnp.float32)
+            for part in kernel_parts
+        ).astype(jnp.bfloat16)
+        kernel_parts = [lax.dynamic_index_in_dim(part, mine, dim, False) for part in kernel_parts]
+        kernel_parts.append(swap(send, "band", 1 << bit))
+    kernel_sum = sum(part.astype(jnp.float32) for part in kernel_parts).reshape(slots, -1)
+    grad_kernel_low = (kernel_sum * band_mask[0].astype(jnp.float32)[:, None]).astype(jnp.bfloat16)
+    range_width = grad_kernel_low.shape[1]
+    hidden_term = lax.dot_general(
+        grad_kernel_low,
+        lax.dynamic_slice_in_dim(gen_w2, band_place * range_width, range_width, 1),
+        (((1,), (1,)), ((), ())),
+        preferred_element_type=jnp.float32,
+    )
+    share = range_width // dp_count
+    kernel_shares = jnp.stack(
+        [
+            lax.dynamic_slice_in_dim(grad_kernel_low, (dp_place ^ i) * share, share, 1)
+            for i in range(dp_count)
+        ]
+    )
+    kernel_rows = in_order(exchange(kernel_shares, "dp"), "dp").reshape(-1, share)
+    gen_w2_grad = lax.dot_general(
+        hidden_all_low,
+        kernel_rows,
+        (((0,), (0,)), ((), ())),
+        preferred_element_type=jnp.float32,
+    )
+
+    small = jnp.concatenate([hidden_term.reshape(-1), ln1_term, ln2_term, sensor_term])
+    for bit in range(bits_of("band")):
+        small = small + swap(small, "band", 1 << bit)
+    all_small = in_order(gather_xor(small, "dp"), "dp")
+    hidden_size = slots * code_width
+    grad_hidden = all_small[:, :hidden_size].reshape(-1, code_width)
+    sums = jnp.sum(all_small[:, hidden_size:], axis=0)
+    ln1_gain_grad = sums[:model_width]
+    ln2_gain_grad = sums[model_width : 2 * model_width]
+    sensor_each = all_small[:, hidden_size + 2 * model_width :]
+    all_pick = (all_tags[None, :] == jnp.arange(sensors, dtype=jnp.int32)[:, None]).astype(
+        jnp.float32
+    )
+    sensor_grad = jnp.dot(all_pick, sensor_each, precision=highest)
+    wave_table_grad, gen_w1_grad = gen_pull(grad_hidden)
+
+    pixel_terms = lax.dot_general(
+        kernel,
+        grad_embed,
+        (((1,), (1,)), ((), ())),
+        preferred_element_type=jnp.float32,
+    )
+    grad_pixels = jnp.zeros((part_rows, band_count * tok_dev), jnp.float32)
+    for mask in range(band_count):
+        other = band_place ^ mask
+        piece = lax.dynamic_slice_in_dim(pixel_terms, other * part_rows, part_rows, 0)
+        if mask:
+            piece = swap(piece.astype(jnp.bfloat16), "band", mask).astype(jnp.float32)
+        grad_pixels = lax.dynamic_update_slice_in_dim(grad_pixels, piece, other * tok_dev, 1)
+    grad_pixels = grad_pixels.reshape(slots_dev, patch_pixels, -1).transpose(0, 2, 1)
+
+    dims = all_bits()
+    core_first = [("band", 0)]
+    rest = [item for item in dims if item not in core_first]
+    fc2_grad = scatter_sum(fc2_term, core_first + rest)
+    turned = core_first + rest[len(rest) // 2 :] + rest[: len(rest) // 2]
+    fc1_grad = scatter_sum(fc1_term, turned).T
+    proj_grad = scatter_sum(proj_term, core_first + rest).T
+    qkv_grad = scatter_sum(qkv_term, core_first + rest).T
     return (
         encoded,
         grad_pixels,

time: 1320 us -> 572 us (0.43)
  waiting for transfers between devices: 860 us -> 107 us
  blocking collectives: 40.7 us -> 0 us
  matrix products: 296 us -> 260 us
  starting transfers between devices: 1.01 us -> 37 us
  other arithmetic: 80.2 us -> 109 us
  local copies, waits for them, and re-layouts: 26.3 us -> 51.8 us
  between operations: 16.1 us -> 2.64 us
    reduce_scatter x6 -> x0, waiting for transfers between devices: 707 us -> none  [the longest x1 253 us: shards(): lax.psum_scatter(gen_w2_term, ('band', 'dp'), scatter_dimension=1, tiled=...]
    psum x1 -> x0, waiting for transfers between devices: 124 us -> none  [shards(): lax.psum((ln1_term, ln2_term, sensor_term, table_term, gen_w1_term), ('ba...]
    ppermute x0 -> x39, waiting for transfers between devices: none -> 107 us  [swap(): return lax.ppermute(piece, axis, [(i, i ^ mask) for i in range(count)])]
    psum x1 -> x0, blocking collectives: 40.7 us -> none  [shards(): lax.psum((ln1_term, ln2_term, sensor_term, table_term, gen_w1_term), ('ba...]
    ppermute x0 -> x39, starting transfers between devices: none -> 37 us  [swap(): return lax.ppermute(piece, axis, [(i, i ^ mask) for i in range(count)])]
    all_gather x1 -> x0, waiting for transfers between devices: 28.8 us -> none  [shards(): piece = lax.all_gather(grad_embed, 'band', axis=0, tiled=True)]
    dot_general x10 -> x11, matrix products: 70.3 us -> 41.8 us  [the longest x1 11.7 us: shards(): jnp.dot(act_low.T, out_grad, preferred_element_type=jnp.float32)]
    convert_element_type x2 -> x19, other arithmetic: 1.42 us -> 20.4 us  [the longest x16 19.7 us: scatter_sum(): send = sum((lax.dynamic_index_in_dim(part, 1 - mine, dim, False).astype(j...]
  transfers between devices with their start and end apart: 8 -> 39, of which waited for: 7 -> 20; matrix products, arithmetic and copies ran while one was open for 7% -> 15% of each run, Pallas kernels for 0% -> 0%
where the time goes in v1:
time: 572 us; the launch traced here: 567 us
  matrix products  260 us (45%)
  other arithmetic  109 us (19%)
  waiting for transfers between devices  107 us (19%)
  local copies, waits for them, and re-layouts  51.8 us (9%)
  starting transfers between devices  37 us (6%)
    ppermute x39, waiting for transfers between devices, swap(): return lax.ppermute(piece, axis, [(i, i ^ mask) for i in range(count)])  107 us
    convert_element_type x1, other arithmetic, attend_back(): grad_scores = (weights * (grad_weights - jnp.sum(weights * grad_weights,...  43.1 us
    dot_general x2, matrix products, attend_back(): jnp.einsum('qhd,khd->hqk', grad_heads[first_row:rows_end], value_heads, p...  37.8 us
    ppermute x39, starting transfers between devices, swap(): return lax.ppermute(piece, axis, [(i, i ^ mask) for i in range(count)])  37 us
    dot_general x2, matrix products, attend_back(): jnp.einsum('hqk,qhd->khd', weights_low, grad_heads[first_row:rows_end], p...  26.3 us
    dot_general x2, matrix products, score_block(): jnp.einsum('qhd,khd->hqk', query_heads, key_heads, preferred_element_type...  25.1 us
    dot_general x2, matrix products, attend_forward(): jnp.einsum('hqk,khd->qhd', weights_low, value_heads, preferred_element_ty...  24.5 us
    reduce_sum x2, other arithmetic, attend_forward(): jnp.sum(jnp.exp(scores - row_peak), axis=-1, keepdims=True)  24 us
  transfers between devices with their start and end apart: 39, of which 20 were waited for; matrix products, arithmetic and copies ran while one was open for 15% of the time, Pallas kernels for 0%

profile of v1, /device:TPU:0, one launch (start us, length us, event | category | flops | bytes accessed | tf_op | source)
XLA Modules:
  0.0 567.4 jit_solution(5364717628669655030)
XLA Ops:
  2.9 3.0 collective-permute-start.6
  12.4 7.3 %fusion = bf16[8,49152]{1,0:T(8,128)(2,1)} fusion(bf16[128,49152]{1,0:T(8,128)(2,1)} %param.23, bf16[8]{0:T(256)(128)(2,1)} %get-tuple-element.143, f32[8,128]{1,0:T(8,128)S(1)} %fusion.93, bf16[128,128]{1,0:T(8,128)(2,1)} %param.22), kind=kOutput, calls=%fused_computation.1 | convolution fusion | flops 102902784 | bytes 13406224 | tf_op jit(solution)/shard_map/dot_general | solution.py:267
  22.2 2.8 copy.81
  32.3 2.6 collective-permute-start.8
  47.1 2.5 add_reduce_fusion
  50.4 4.5 convolution_convert_fusion.1
  58.1 2.6 copy.78
  65.3 2.6 copy.76
  67.9 14.4 %fusion.2 = (f32[12,512]{1,0:T(8,128)S(1)}, f32[12,512,1024]{2,1,0:T(8,128)}) fusion(pred[512,1024]{1,0:T(8,128)(4,1)} %get-tuple-element.139, bf16[512,12,64]{0,2,1:T(8,128)(2,1)} %bitcast.432, bf16[1024,12,64]{0,2,1:T(8,128)(2,1)} %bitcast.424), kind=kOutput, calls=%fused_computation.13 | convolution fusion | flops 824174592 | bytes 28073984 | tf_op jit(solution)/shard_map/while/body/eval_jaxpr/qhd,khd->hqk/dot_general | solution.py:38
  82.3 12.1 %exponential_reduce_fusion = f32[12,512]{1,0:T(8,128)S(1)} fusion(f32[12,512,1024]{2,1,0:T(8,128)} %get-tuple-element.147, f32[12,512]{1,0:T(8,128)S(1)} %get-tuple-element.146, pred[512,1024]{1,0:T(8,128)(4,1)S(1)} %copy-done.4), kind=kLoop, calls=%fused_computation.7 | loop fusion | flops 25159680 | bytes 25739264 | tf_op jit(solution)/shard_map/while/body/eval_jaxpr/reduce_sum | solution.py:65
  94.5 10.7 %fusion.1 = (f32[12,512]{1,0:T(8,128)S(1)}, f32[12,512,1024]{2,1,0:T(8,128)}) fusion(pred[512,1024]{1,0:T(8,128)(4,1)S(1)} %copy-done.6, bf16[512,12,64]{0,2,1:T(8,128)(2,1)S(1)} %bitcast.434, bf16[1024,12,64]{0,2,1:T(8,128)(2,1)S(1)} %bitcast.425), kind=kOutput, calls=%fused_computation.12 | convolution fusion | flops 824174592 | bytes 28073984 | tf_op jit(solution)/shard_map/while/body/eval_jaxpr/qhd,khd->hqk/dot_general | solution.py:38
  105.2 11.9 %exponential_reduce_fusion.1 = f32[12,512]{1,0:T(8,128)S(1)} fusion(f32[12,512,1024]{2,1,0:T(8,128)} %get-tuple-element.149, f32[12,512]{1,0:T(8,128)S(1)} %get-tuple-element.148, pred[512,1024]{1,0:T(8,128)(4,1)S(1)} %copy-done.6), kind=kLoop, calls=%fused_computation.10 | loop fusion | flops 25159680 | bytes 25739264 | tf_op jit(solution)/shard_map/while/body/eval_jaxpr/reduce_sum | solution.py:65
  117.1 12.0 %convolution_convert_fusion.8 = bf16[12,64,512]{2,1,0:T(8,128)(2,1)} fusion(bf16[1024,12,64]{0,2,1:T(8,128)(2,1)S(1)} %bitcast.430, f32[12,512,1024]{2,1,0:T(8,128)} %get-tuple-element.147, f32[12,512]{1,0:T(8,128)S(1)} %log_add_fusion, pred[512,1024]{1,0:T(8,128)(4,1)S(1)} %copy-done.4), kind=kOutput, calls=%fused_computation.67 | convolution fusion | flops 830865408 | bytes 28073984 | tf_op jit(solution)/shard_map/while/body/eval_jaxpr/hqk,khd->qhd/dot_general | solution.py:67
  129.1 12.5 %convolution_convert_fusion.9 = bf16[12,64,512]{2,1,0:T(8,128)(2,1)} fusion(bf16[1024,12,64]{0,2,1:T(8,128)(2,1)S(1)} %bitcast.431, f32[12,512,1024]{2,1,0:T(8,128)} %get-tuple-element.149, f32[12,512]{1,0:T(8,128)S(1)} %log_add_fusion.1, pred[512,1024]{1,0:T(8,128)(4,1)S(1)} %copy-done.6), kind=kOutput, calls=%fused_computation.68 | convolution fusion | flops 830865408 | bytes 28073984 | tf_op jit(solution)/shard_map/while/body/eval_jaxpr/hqk,khd->qhd/dot_general | solution.py:67
  141.6 3.6 fusion.144
  145.9 8.5 %fusion.135 = f32[1024,3072]{1,0:T(8,128)} fusion(bf16[768,3072]{1,0:T(8,128)(2,1)S(1)} %bitcast.437, f32[1024,768]{0,1:T(8,128)S(1)} %get-tuple-element.151, f32[768]{0:T(1024)S(1)} %copy-done.26, f32[1024]{0:T(1024)S(1)} %add_rsqrt_fusion, f32[1024]{0:T(1024)S(1)} %broadcast_multiply_fusion.4), kind=kOutput, calls=%fused_computation.335 | convolution fusion | flops 4834983936 | bytes 20458496 | tf_op jit(solution)/shard_map/dot_general | solution.py:295
  154.4 11.7 %convolution_convert_fusion.2 = bf16[3072,768]{1,0:T(8,128)(2,1)} fusion(bf16[1024,768]{1,0:T(8,128)(2,1)S(1)} %copy-done.20, f32[1024,3072]{1,0:T(8,128)} %fusion.135), kind=kOutput, calls=%fused_computation.27 | convolution fusion | flops 4862509056 | bytes 18874368 | tf_op jit(solution)/shard_map/dot_general | solution.py:299
  166.1 11.6 %convolution_add_fusion = f32[1024,768]{0,1:T(8,128)} fusion(f32[1024,768]{0,1:T(8,128)S(1)} %get-tuple-element.151, bf16[3072,768]{1,0:T(8,128)(2,1)} %param.30, f32[1024,3072]{1,0:T(8,128)} %fusion.135), kind=kOutput, calls=%fused_computation.60 | convolution fusion | flops 4860936192 | bytes 23592960 | tf_op jit(solution)/shard_map/dot_general | solution.py:297
  177.7 15.4 %fusion.11 = bf16[1024,3072]{1,0:T(8,128)(2,1)} fusion(f32[1024,3072]{1,0:T(8,128)} %fusion.135, bf16[1024,768]{1,0:T(8,128)(2,1)S(1)} %copy-done.20, bf16[3072,768]{1,0:T(8,128)(2,1)} %param.30), kind=kOutput, calls=%fused_computation.24 | convolution fusion | flops 4894752768 | bytes 25165824 | tf_op jit(solution)/shard_map/dot_general | solution.py:298
  193.1 8.8 %multiply_reduce_fusion.2 = (f32[768]{0:T(1024)}, f32[1024]{0:T(1024)S(1)}, f32[1024]{0:T(1024)S(1)}, f32[1024,768]{0,1:T(8,128)S(1)}) fusion(f32[1024,768]{0,1:T(8,128)S(1)} %get-tuple-element.151, f32[1024]{0:T(1024)S(1)} %add_rsqrt_fusion, f32[1024]{0:T(1024)S(1)} %broadcast_multiply_fusion.4, f32[768]{0:T(1024)S(1)} %copy-done.26, ...), kind=kOutput, calls=%fused_computation.31 | convolution fusion | flops 4838126592 | bytes 17324032 | tf_op jit(solution)/shard_map/dot_general | solution.py:305
  201.9 7.3 %convolution_convert_fusion.3 = bf16[3072,768]{1,0:T(8,128)(2,1)} fusion(bf16[1024,3072]{1,0:T(8,128)(2,1)S(1)} %copy-done.50, f32[1024,768]{0,1:T(8,128)S(1)} %get-tuple-element.151, f32[768]{0:T(1024)S(1)} %copy-done.26, f32[1024]{0:T(1024)S(1)} %add_rsqrt_fusion, f32[1024]{0:T(1024)S(1)} %broadcast_multiply_fusion.4), kind=kOutput, calls=%fused_computation.28 | convolution fusion | flops 4837343232 | bytes 14167040 | tf_op jit(solution)/shard_map/dot_general | solution.py:302
  216.4 13.4 %fusion.56 = f32[12,64,1024]{2,1,0:T(8,128)} fusion(bf16[512,12,64]{0,2,1:T(8,128)(2,1)S(1)} %bitcast.460, f32[12,512,1024]{2,1,0:T(8,128)} %get-tuple-element.149, f32[12,512]{1,0:T(8,128)S(1)} %log_add_fusion.1, pred[512,1024]{1,0:T(8,128)(4,1)S(1)} %copy-done.6), kind=kOutput, calls=%fused_computation.183 | convolution fusion | flops 830472192 | bytes 29646848 | tf_op jit(solution)/shard_map/while/body/eval_jaxpr/hqk,qhd->khd/dot_general | solution.py:123
  229.7 18.9 %multiply_reduce_fusion.1 = (f32[12,512]{1,0:T(8,128)}, f32[12,512,1024]{2,1,0:T(8,128)}) fusion(f32[12,512,1024]{2,1,0:T(8,128)} %get-tuple-element.149, f32[12,512]{1,0:T(8,128)} %copy-done.29, pred[512,1024]{1,0:T(8,128)(4,1)} %get-tuple-element.138, bf16[512,12,64]{0,2,1:T(8,128)(2,1)} %bitcast.461, bf16[1024,12,64]{0,2,1:T(8,128)(2,1)} %bitcast.428), kind=kOutput, calls=%fused_computation.5 | convolution fusion | flops 836757504 | bytes 53264384 | tf_op jit(solution)/shard_map/while/body/eval_jaxpr/qhd,khd->hqk/dot_general | solution.py:98
  248.7 18.9 %multiply_reduce_fusion = (f32[12,512]{1,0:T(8,128)}, f32[12,512,1024]{2,1,0:T(8,128)}) fusion(f32[12,512,1024]{2,1,0:T(8,128)} %get-tuple-element.147, f32[12,512]{1,0:T(8,128)} %copy-done.27, pred[512,1024]{1,0:T(8,128)(4,1)} %get-tuple-element.139, bf16[512,12,64]{0,2,1:T(8,128)(2,1)} %bitcast.458, bf16[1024,12,64]{0,2,1:T(8,128)(2,1)} %bitcast.429), kind=kOutput, calls=%fused_computation.3 | convolution fusion | flops 836757504 | bytes 53264384 | tf_op jit(solution)/shard_map/while/body/eval_jaxpr/qhd,khd->hqk/dot_general | solution.py:98
  267.6 43.1 %multiply_convert_fusion = (bf16[12,512,1024]{2,1,0:T(8,128)(2,1)}, bf16[12,512,1024]{2,1,0:T(8,128)(2,1)}) fusion(f32[12,512,1024]{2,1,0:T(8,128)} %get-tuple-element.156, f32[12,512,1024]{2,1,0:T(8,128)} %get-tuple-element.147, f32[12,512]{1,0:T(8,128)} %get-tuple-element.155, f32[12,512]{1,0:T(8,128)} %copy-done.27, ...), kind=kLoop, calls=%fused_computation.2 | loop fusion | flops 75497472 | bytes 126976000 | tf_op jit(solution)/shard_map/while/body/eval_jaxpr/convert_element_type | solution.py:106
  310.7 8.7 %multiply_convert_fusion.7 = bf16[12,64,512]{2,1,0:T(8,128)(2,1)S(1)} fusion(bf16[1024,12,64]{0,2,1:T(8,128)(2,1)S(1)} %bitcast.426, bf16[12,512,1024]{2,1,0:T(8,128)(2,1)} %get-tuple-element.159), kind=kOutput, calls=%fused_computation.64 | convolution fusion | flops 806092800 | bytes 14942208 | tf_op jit(solution)/shard_map/while/body/eval_jaxpr/hqk,khd->qhd/dot_general | solution.py:108
  319.4 7.0 %fusion.145 = f32[12,64,1024]{2,1,0:T(8,128)S(1)} fusion(bf16[512,12,64]{0,2,1:T(8,128)(2,1)S(1)} %bitcast.435, bf16[12,512,1024]{2,1,0:T(8,128)(2,1)} %get-tuple-element.159), kind=kOutput, calls=%fused_computation.345 | convolution fusion | flops 805306368 | bytes 16515072 | tf_op jit(solution)/shard_map/while/body/eval_jaxpr/hqk,qhd->khd/dot_general | solution.py:115
  326.4 13.0 %add_convert_fusion = bf16[12,64,1024]{2,1,0:T(8,128)(2,1)S(1)} fusion(f32[12,64,1024]{2,1,0:T(8,128)} %fusion.56, bf16[512,12,64]{0,2,1:T(8,128)(2,1)S(1)} %bitcast.459, f32[12,512,1024]{2,1,0:T(8,128)} %get-tuple-element.147, f32[12,512]{1,0:T(8,128)S(1)} %copy-done.28, pred[512,1024]{1,0:T(8,128)(4,1)S(1)} %copy-done.5), kind=kOutput, calls=%fused_computation.37 | convolution fusion | flops 832045056 | bytes 31219712 | tf_op jit(solution)/shard_map/while/body/eval_jaxpr/hqk,qhd->khd/dot_general | solution.py:123
  339.4 8.7 %multiply_convert_fusion.6 = bf16[12,64,512]{2,1,0:T(8,128)(2,1)S(1)} fusion(bf16[1024,12,64]{0,2,1:T(8,128)(2,1)S(1)} %bitcast.427, bf16[12,512,1024]{2,1,0:T(8,128)(2,1)} %get-tuple-element.158), kind=kOutput, calls=%fused_computation.63 | convolution fusion | flops 806092800 | bytes 14942208 | tf_op jit(solution)/shard_map/while/body/eval_jaxpr/hqk,khd->qhd/dot_general | solution.py:108
  348.1 7.0 %multiply_convert_fusion.3 = bf16[12,64,1024]{2,1,0:T(8,128)(2,1)S(1)} fusion(f32[12,64,1024]{2,1,0:T(8,128)S(1)} %fusion.145, bf16[512,12,64]{0,2,1:T(8,128)(2,1)S(1)} %bitcast.433, bf16[12,512,1024]{2,1,0:T(8,128)(2,1)} %get-tuple-element.158), kind=kOutput, calls=%fused_computation.38 | convolution fusion | flops 807665664 | bytes 18087936 | tf_op jit(solution)/shard_map/while/body/eval_jaxpr/hqk,qhd->khd/dot_general | solution.py:115
  355.2 4.4 multiply_reduce_fusion.3
  359.6 6.0 %convolution_convert_fusion.4 = bf16[2304,768]{1,0:T(8,128)(2,1)} fusion(bf16[1024,768]{0,1:T(8,128)(2,1)S(1)} %bitcast.498, bf16[1024,768]{0,1:T(8,128)(2,1)S(1)} %bitcast.451, bf16[512,768]{0,1:T(8,128)(2,1)S(1)} %bitcast.473, bf16[512,768]{0,1:T(8,128)(2,1)S(1)} %bitcast.471, f32[768]{0:T(1024)S(1)} %copy-done.42, f32[1024,768]{0,1:T(8,128)S(1)} %copy-done.9, ...), kind=kOutput, calls=%fused_computation.29 | convolution fusion | flops 3648454656 | bytes 11417600 | tf_op jit(solution)/shard_map/dot_general | solution.py:331
  367.9 3.2 convolution_convert_fusion.7
  373.4 3.5 copy.96
  377.0 3.4 dynamic-slice_bitcast_fusion
  381.0 3.4 dynamic-slice_bitcast_fusion.1
  395.8 6.1 %collective-permute-done.5 = bf16[128,1024]{1,0:T(8,128)(2,1)S(1)} collective-permute-done((bf16[128,1024]{1,0:T(8,128)(2,1)S(1)}, bf16[128,1024]{1,0:T(8,128)(2,1)S(1)}, u32[]{:S(2)}, u32[]{:S(2)}) %collective-permute-start.5) | collective-permute-done | bytes 262176 | tf_op jit(solution)/shard_map/ppermute | solution.py:141
  405.5 4.1 collective-permute-done.10
  410.1 2.8 fusion.19
  418.1 3.7 collective-permute-done.13
  425.8 4.5 collective-permute-done.16
  430.3 2.6 collective-permute-start.15
  450.7 3.0 collective-permute-start.18
  464.8 34.4 %collective-permute-done.20 = bf16[2,2,2,72,768]{4,3,2,1,0:T(8,128)(2,1)S(1)} collective-permute-done((bf16[2,2,2,72,768]{4,3,2,1,0:T(8,128)(2,1)S(1)}, bf16[2,2,2,72,768]{4,3,2,1,0:T(8,128)(2,1)S(1)}, u32[]{:S(2)}, u32[]{:S(2)}) %collective-permute-start.20) | collective-permute-done | bytes 884768 | tf_op jit(solution)/shard_map/ppermute | solution.py:141
  509.2 9.1 %collective-permute-done.27 = bf16[2,24,768]{2,1,0:T(8,128)(2,1)S(1)} collective-permute-done((bf16[2,24,768]{2,1,0:T(8,128)(2,1)S(1)}, bf16[2,24,768]{2,1,0:T(8,128)(2,1)S(1)}, u32[]{:S(2)}, u32[]{:S(2)}) %collective-permute-start.27) | collective-permute-done | bytes 73760 | tf_op jit(solution)/shard_map/ppermute | solution.py:141
  519.7 7.2 %collective-permute-done.21 = bf16[2,2,72,768]{3,2,1,0:T(8,128)(2,1)S(1)} collective-permute-done((bf16[2,2,72,768]{3,2,1,0:T(8,128)(2,1)S(1)}, bf16[2,2,72,768]{3,2,1,0:T(8,128)(2,1)S(1)}, u32[]{:S(2)}, u32[]{:S(2)}) %collective-permute-start.21) | collective-permute-done | bytes 442400 | tf_op jit(solution)/shard_map/ppermute | solution.py:141
  528.9 10.7 %collective-permute-done.36 = bf16[2,2,96,768]{3,2,1,0:T(8,128)(2,1)S(1)} collective-permute-done((bf16[2,2,96,768]{3,2,1,0:T(8,128)(2,1)S(1)}, bf16[2,2,96,768]{3,2,1,0:T(8,128)(2,1)S(1)}, u32[]{:S(2)}, u32[]{:S(2)}) %collective-permute-start.36) | collective-permute-done | bytes 589856 | tf_op jit(solution)/shard_map/ppermute | solution.py:141
  559.3 6.0 %collective-permute-done.33 = bf16[96,768]{1,0:T(8,128)(2,1)S(1)} collective-permute-done((bf16[96,768]{1,0:T(8,128)(2,1)S(1)}, bf16[96,768]{1,0:T(8,128)(2,1)S(1)}, u32[]{:S(2)}, u32[]{:S(2)}) %collective-permute-start.33) | collective-permute-done | bytes 147488 | tf_op jit(solution)/shard_map/ppermute | solution.py:141
  (288 shorter events, 139.9 us)
Async XLA Ops:
  0.6 49.5 %copy-start = (bf16[768,2304]{1,0:T(8,128)(2,1)S(1)}, bf16[768,2304]{1,0:T(8,128)(2,1)}, u32[]{:S(2)}) copy-start(bf16[768,2304]{1,0:T(8,128)(2,1)} %param.26) | copy-start | bytes 10616836
  2.9 24.5 %collective-permute-start.6 = (s32[1,17]{1,0:T(1,128)}, s32[1,17]{1,0:T(1,128)}, u32[]{:S(2)}, u32[]{:S(2)}) collective-permute-start(s32[1,17]{1,0:T(1,128)} %add_bitcast_fusion), channel_id=1, source_target_pairs={{0,1},{1,0},{2,3},{3,2},{4,5},{5,4},{6,7},{7,6},{8,9},{9,8},{10,11... | collective-permute-start | bytes 212 | tf_op jit(solution)/shard_map/ppermute | solution.py:141
  9.1 36.3 %collective-permute-start.2 = (bf16[128,1024]{1,0:T(8,128)(2,1)}, bf16[128,1024]{1,0:T(8,128)(2,1)}, u32[]{:S(2)}, u32[]{:S(2)}) collective-permute-start(bf16[128,1024]{1,0:T(8,128)(2,1)} %get-tuple-element.110), channel_id=1, source_target_pairs={{0,24},{8,16},{16,8},{24,0},{1,25},{9,17},{17,9},{25,1},{2,26},{10... | collective-permute-start | bytes 786440 | tf_op jit(solution)/shard_map/ppermute | solution.py:141
  9.8 33.9 %collective-permute-start.1 = (bf16[128,1024]{1,0:T(8,128)(2,1)}, bf16[128,1024]{1,0:T(8,128)(2,1)}, u32[]{:S(2)}, u32[]{:S(2)}) collective-permute-start(bf16[128,1024]{1,0:T(8,128)(2,1)} %get-tuple-element.111), channel_id=1, source_target_pairs={{0,16},{8,24},{16,0},{24,8},{1,17},{9,25},{17,1},{25,9},{2,18},{10... | collective-permute-start | bytes 786440 | tf_op jit(solution)/shard_map/ppermute | solution.py:141
  10.7 31.4 %collective-permute-start = (bf16[128,1024]{1,0:T(8,128)(2,1)}, bf16[128,1024]{1,0:T(8,128)(2,1)}, u32[]{:S(2)}, u32[]{:S(2)}) collective-permute-start(bf16[128,1024]{1,0:T(8,128)(2,1)} %get-tuple-element.112), channel_id=1, source_target_pairs={{0,8},{8,0},{16,24},{24,16},{1,9},{9,1},{17,25},{25,17},{2,10},{10... | collective-permute-start | bytes 786440 | tf_op jit(solution)/shard_map/ppermute | solution.py:141
  25.8 115.9 %copy-start.35 = (f32[768]{0:T(1024)}, f32[768]{0:T(1024)S(1)}, u32[]{:S(2)}) copy-start(f32[768]{0:T(1024)S(1)} %convolution_reduce_fusion) | copy-start | bytes 9220
  28.1 3.6 collective-permute-start.7
  32.3 4.5 collective-permute-start.8
  94.4 22.6 %copy-start.27 = (f32[12,512]{1,0:T(8,128)}, f32[12,512]{1,0:T(8,128)S(1)}, u32[]{:S(2)}) copy-start(f32[12,512]{1,0:T(8,128)S(1)} %log_add_fusion) | copy-start | bytes 73732
  117.1 98.4 %copy-start.29 = (f32[12,512]{1,0:T(8,128)}, f32[12,512]{1,0:T(8,128)S(1)}, u32[]{:S(2)}) copy-start(f32[12,512]{1,0:T(8,128)S(1)} %log_add_fusion.1) | copy-start | bytes 73732
  267.6 43.1 %copy-start.2 = (bf16[1024,768]{0,1:T(8,128)(2,1)S(1)}, bf16[1024,768]{0,1:T(8,128)(2,1)}, u32[]{:S(2)}) copy-start(bf16[1024,768]{0,1:T(8,128)(2,1)} %copy.78) | copy-start | bytes 4718596
  380.4 76.8 %collective-permute-start.34 = (bf16[2,2,2,2,96,768]{5,4,3,2,1,0:T(8,128)(2,1)}, bf16[2,2,2,2,96,768]{5,4,3,2,1,0:T(8,128)(2,1)}, u32[]{:S(2)}, u32[]{:S(2)}) collective-permute-start(bf16[2,2,2,2,96,768]{5,4,3,2,1,0:T(8,128)(2,1)} %dynamic-slice_bitcast_fusion), channel_id=1, source_target_pairs={{0,8},{8,0},{16,24},{24,16},{1,9},{9,1},{17,25},{25,17},{2,10},{10... | collective-permute-start | bytes 7077896 | tf_op jit(solution)/shard_map/ppermute | solution.py:141
  380.5 23.7 %collective-permute-start.24 = (bf16[2,2,2,2,24,768]{5,4,3,2,1,0:T(8,128)(2,1)S(1)}, bf16[2,2,2,2,24,768]{5,4,3,2,1,0:T(8,128)(2,1)S(1)}, u32[]{:S(2)}, u32[]{:S(2)}) collective-permute-start(bf16[2,2,2,2,24,768]{5,4,3,2,1,0:T(8,128)(2,1)S(1)} %dynamic-slice_bitcast_fusion.3), channel_id=1, source_target_pairs={{0,8},{8,0},{16,24},{24,16},{1,9},{9,1},{17,25},{25,17},{2,10},{10... | collective-permute-start | bytes 1769480 | tf_op jit(solution)/shard_map/ppermute | solution.py:141
  384.4 78.3 %collective-permute-start.29 = (bf16[2,2,2,2,96,768]{5,4,3,2,1,0:T(8,128)(2,1)}, bf16[2,2,2,2,96,768]{5,4,3,2,1,0:T(8,128)(2,1)}, u32[]{:S(2)}, u32[]{:S(2)}) collective-permute-start(bf16[2,2,2,2,96,768]{5,4,3,2,1,0:T(8,128)(2,1)} %dynamic-slice_bitcast_fusion.1), channel_id=1, source_target_pairs={{0,8},{8,0},{16,24},{24,16},{1,9},{9,1},{17,25},{25,17},{2,10},{10... | collective-permute-start | bytes 7077896 | tf_op jit(solution)/shard_map/ppermute | solution.py:141
  384.6 8.8 %collective-permute-start.4 = (bf16[128,1024]{1,0:T(8,128)(2,1)S(1)}, bf16[128,1024]{1,0:T(8,128)(2,1)S(1)}, u32[]{:S(2)}, u32[]{:S(2)}) collective-permute-start(bf16[128,1024]{1,0:T(8,128)(2,1)S(1)} %get-tuple-element.106), channel_id=1, source_target_pairs={{0,16},{8,24},{16,0},{24,8},{1,17},{9,25},{17,1},{25,9},{2,18},{10... | collective-permute-start | bytes 786440 | tf_op jit(solution)/shard_map/ppermute | solution.py:141
  386.1 3.9 collective-permute-start.3
  390.0 19.9 %copy-start.46 = (f32[8]{0:T(128)S(1)}, f32[8]{0:T(128)}, u32[]{:S(2)}) copy-start(f32[8]{0:T(128)} %get-tuple-element.142) | copy-start | bytes 100
  390.1 4.9 collective-permute-start.9
  393.3 8.6 %collective-permute-start.5 = (bf16[128,1024]{1,0:T(8,128)(2,1)S(1)}, bf16[128,1024]{1,0:T(8,128)(2,1)S(1)}, u32[]{:S(2)}, u32[]{:S(2)}) collective-permute-start(bf16[128,1024]{1,0:T(8,128)(2,1)S(1)} %get-tuple-element.105), channel_id=1, source_target_pairs={{0,24},{8,16},{16,8},{24,0},{1,25},{9,17},{17,9},{25,1},{2,26},{10... | collective-permute-start | bytes 786440 | tf_op jit(solution)/shard_map/ppermute | solution.py:141
  395.0 65.7 %collective-permute-start.19 = (bf16[2,2,2,2,72,768]{5,4,3,2,1,0:T(8,128)(2,1)}, bf16[2,2,2,2,72,768]{5,4,3,2,1,0:T(8,128)(2,1)}, u32[]{:S(2)}, u32[]{:S(2)}) collective-permute-start(bf16[2,2,2,2,72,768]{5,4,3,2,1,0:T(8,128)(2,1)} %dynamic-slice_bitcast_fusion.2), channel_id=1, source_target_pairs={{0,8},{8,0},{16,24},{24,16},{1,9},{9,1},{17,25},{25,17},{2,10},{10... | collective-permute-start | bytes 5308424 | tf_op jit(solution)/shard_map/ppermute | solution.py:141
  401.9 7.8 %collective-permute-start.10 = (bf16[8,16,768]{2,1,0:T(8,128)(2,1)S(1)}, bf16[8,16,768]{2,1,0:T(8,128)(2,1)S(1)}, u32[]{:S(2)}, u32[]{:S(2)}) collective-permute-start(bf16[8,16,768]{2,1,0:T(8,128)(2,1)S(1)} %fusion.33), channel_id=1, source_target_pairs={{0,16},{8,24},{16,0},{24,8},{1,17},{9,25},{17,1},{25,9},{2,18},{10... | collective-permute-start | bytes 589832 | tf_op jit(solution)/shard_map/ppermute | solution.py:141
  404.9 48.7 %collective-permute-start.25 = (bf16[2,2,2,24,768]{4,3,2,1,0:T(8,128)(2,1)}, bf16[2,2,2,24,768]{4,3,2,1,0:T(8,128)(2,1)}, u32[]{:S(2)}, u32[]{:S(2)}) collective-permute-start(bf16[2,2,2,24,768]{4,3,2,1,0:T(8,128)(2,1)} %fusion.31), channel_id=1, source_target_pairs={{0,16},{8,24},{16,0},{24,8},{1,17},{9,25},{17,1},{25,9},{2,18},{10... | collective-permute-start | bytes 884744 | tf_op jit(solution)/shard_map/ppermute | solution.py:141
  412.9 1.2 collective-permute-start.11
  414.2 3.8 collective-permute-start.12
  418.0 3.8 collective-permute-start.13
  421.8 3.9 collective-permute-start.14
  425.7 4.6 collective-permute-start.16
  430.3 5.0 collective-permute-start.15
  435.4 14.3 %collective-permute-start.17 = (bf16[2,2,8,1536]{3,2,0,1:T(8,128)(2,1)}, bf16[2,2,8,1536]{3,2,0,1:T(8,128)(2,1)}, u32[]{:S(2)}, u32[]{:S(2)}) collective-permute-start(bf16[2,2,8,1536]{3,2,0,1:T(8,128)(2,1)} %get-tuple-element.117), channel_id=1, source_target_pairs={{0,2},{1,3},{2,0},{3,1},{4,6},{5,7},{6,4},{7,5},{8,10},{9,11},{10,... | collective-permute-start | bytes 294920 | tf_op jit(solution)/shard_map/ppermute | solution.py:141
  444.2 16.5 %copy-start.17 = (bf16[2304,768]{1,0:T(8,128)(2,1)S(1)}, bf16[2304,768]{1,0:T(8,128)(2,1)}, u32[]{:S(2)}) copy-start(bf16[2304,768]{1,0:T(8,128)(2,1)} %convolution_convert_fusion.4) | copy-start | bytes 10616836
  450.7 6.5 %collective-permute-start.18 = (bf16[1,4,8,1536]{3,2,1,0:T(8,128)(2,1)S(1)}, bf16[1,4,8,1536]{3,2,1,0:T(8,128)(2,1)S(1)}, u32[]{:S(2)}, u32[]{:S(2)}) collective-permute-start(bf16[1,4,8,1536]{3,2,1,0:T(8,128)(2,1)S(1)} %get-tuple-element.115), channel_id=1, source_target_pairs={{0,4},{1,5},{2,6},{3,7},{4,0},{5,1},{6,2},{7,3},{8,12},{9,13},{10,... | collective-permute-start | bytes 294920 | tf_op jit(solution)/shard_map/ppermute | solution.py:141
  454.7 51.4 %collective-permute-start.26 = (bf16[2,2,24,768]{3,2,1,0:T(8,128)(2,1)S(1)}, bf16[2,2,24,768]{3,2,1,0:T(8,128)(2,1)S(1)}, u32[]{:S(2)}, u32[]{:S(2)}) collective-permute-start(bf16[2,2,24,768]{3,2,1,0:T(8,128)(2,1)S(1)} %fusion.41), channel_id=1, source_target_pairs={{0,4},{1,5},{2,6},{3,7},{4,0},{5,1},{6,2},{7,3},{8,12},{9,13},{10,... | collective-permute-start | bytes 442376 | tf_op jit(solution)/shard_map/ppermute | solution.py:141
  459.2 43.2 %collective-permute-start.35 = (bf16[2,2,2,96,768]{4,3,2,1,0:T(8,128)(2,1)S(1)}, bf16[2,2,2,96,768]{4,3,2,1,0:T(8,128)(2,1)S(1)}, u32[]{:S(2)}, u32[]{:S(2)}) collective-permute-start(bf16[2,2,2,96,768]{4,3,2,1,0:T(8,128)(2,1)S(1)} %fusion.14), channel_id=1, source_target_pairs={{0,16},{8,24},{16,0},{24,8},{1,17},{9,25},{17,1},{25,9},{2,18},{10... | collective-permute-start | bytes 3538952 | tf_op jit(solution)/shard_map/ppermute | solution.py:141
  462.1 37.1 %collective-permute-start.20 = (bf16[2,2,2,72,768]{4,3,2,1,0:T(8,128)(2,1)S(1)}, bf16[2,2,2,72,768]{4,3,2,1,0:T(8,128)(2,1)S(1)}, u32[]{:S(2)}, u32[]{:S(2)}) collective-permute-start(bf16[2,2,2,72,768]{4,3,2,1,0:T(8,128)(2,1)S(1)} %fusion.16), channel_id=1, source_target_pairs={{0,16},{8,24},{16,0},{24,8},{1,17},{9,25},{17,1},{25,9},{2,18},{10... | collective-permute-start | bytes 2654216 | tf_op jit(solution)/shard_map/ppermute | solution.py:141
  462.7 42.2 %copy-start.31 = (f32[64,128]{1,0:T(8,128)S(1)}, f32[64,128]{1,0:T(8,128)}, u32[]{:S(2)}) copy-start(f32[64,128]{1,0:T(8,128)} %copy-done.30) | copy-start | bytes 98308
  462.7 42.2 %copy-start.32 = (f32[64,128]{1,0:T(8,128)S(1)}, f32[64,128]{1,0:T(8,128)}, u32[]{:S(2)}) copy-start(f32[64,128]{1,0:T(8,128)} %fusion.146) | copy-start | bytes 98308
  464.7 42.5 %collective-permute-start.30 = (bf16[2,2,2,96,768]{4,3,2,1,0:T(8,128)(2,1)S(1)}, bf16[2,2,2,96,768]{4,3,2,1,0:T(8,128)(2,1)S(1)}, u32[]{:S(2)}, u32[]{:S(2)}) collective-permute-start(bf16[2,2,2,96,768]{4,3,2,1,0:T(8,128)(2,1)S(1)} %fusion.15), channel_id=1, source_target_pairs={{0,2},{1,3},{2,0},{3,1},{4,6},{5,7},{6,4},{7,5},{8,10},{9,11},{10,... | collective-permute-start | bytes 3538952 | tf_op jit(solution)/shard_map/ppermute | solution.py:141
  500.4 26.6 %collective-permute-start.21 = (bf16[2,2,72,768]{3,2,1,0:T(8,128)(2,1)S(1)}, bf16[2,2,72,768]{3,2,1,0:T(8,128)(2,1)S(1)}, u32[]{:S(2)}, u32[]{:S(2)}) collective-permute-start(bf16[2,2,72,768]{3,2,1,0:T(8,128)(2,1)S(1)} %fusion.22), channel_id=1, source_target_pairs={{0,4},{1,5},{2,6},{3,7},{4,0},{5,1},{6,2},{7,3},{8,12},{9,13},{10,... | collective-permute-start | bytes 1327112 | tf_op jit(solution)/shard_map/ppermute | solution.py:141
  503.9 35.7 %collective-permute-start.36 = (bf16[2,2,96,768]{3,2,1,0:T(8,128)(2,1)S(1)}, bf16[2,2,96,768]{3,2,1,0:T(8,128)(2,1)S(1)}, u32[]{:S(2)}, u32[]{:S(2)}) collective-permute-start(bf16[2,2,96,768]{3,2,1,0:T(8,128)(2,1)S(1)} %fusion.17), channel_id=1, source_target_pairs={{0,4},{1,5},{2,6},{3,7},{4,0},{5,1},{6,2},{7,3},{8,12},{9,13},{10,... | collective-permute-start | bytes 1769480 | tf_op jit(solution)/shard_map/ppermute | solution.py:141
  507.1 11.2 %collective-permute-start.27 = (bf16[2,24,768]{2,1,0:T(8,128)(2,1)S(1)}, bf16[2,24,768]{2,1,0:T(8,128)(2,1)S(1)}, u32[]{:S(2)}, u32[]{:S(2)}) collective-permute-start(bf16[2,24,768]{2,1,0:T(8,128)(2,1)S(1)} %fusion.47), channel_id=1, source_target_pairs={{0,2},{1,3},{2,0},{3,1},{4,6},{5,7},{6,4},{7,5},{8,10},{9,11},{10,... | collective-permute-start | bytes 221192 | tf_op jit(solution)/shard_map/ppermute | solution.py:141
  508.7 37.5 %collective-permute-start.31 = (bf16[2,2,96,768]{3,2,1,0:T(8,128)(2,1)S(1)}, bf16[2,2,96,768]{3,2,1,0:T(8,128)(2,1)S(1)}, u32[]{:S(2)}, u32[]{:S(2)}) collective-permute-start(bf16[2,2,96,768]{3,2,1,0:T(8,128)(2,1)S(1)} %fusion.18), channel_id=1, source_target_pairs={{0,1},{1,0},{2,3},{3,2},{4,5},{5,4},{6,7},{7,6},{8,9},{9,8},{10,11... | collective-permute-start | bytes 1769480 | tf_op jit(solution)/shard_map/ppermute | solution.py:141
  519.2 21.7 %collective-permute-start.28 = (bf16[24,768]{1,0:T(8,128)(2,1)S(1)}, bf16[24,768]{1,0:T(8,128)(2,1)S(1)}, u32[]{:S(2)}, u32[]{:S(2)}) collective-permute-start(bf16[24,768]{1,0:T(8,128)(2,1)S(1)} %fusion.51), channel_id=1, source_target_pairs={{0,1},{1,0},{2,3},{3,2},{4,5},{5,4},{6,7},{7,6},{8,9},{9,8},{10,11... | collective-permute-start | bytes 110600 | tf_op jit(solution)/shard_map/ppermute | solution.py:141
  528.0 16.3 %collective-permute-start.22 = (bf16[2,72,768]{2,1,0:T(8,128)(2,1)S(1)}, bf16[2,72,768]{2,1,0:T(8,128)(2,1)S(1)}, u32[]{:S(2)}, u32[]{:S(2)}) collective-permute-start(bf16[2,72,768]{2,1,0:T(8,128)(2,1)S(1)} %fusion.32), channel_id=1, source_target_pairs={{0,2},{1,3},{2,0},{3,1},{4,6},{5,7},{6,4},{7,5},{8,10},{9,11},{10,... | collective-permute-start | bytes 663560 | tf_op jit(solution)/shard_map/ppermute | solution.py:141
  540.8 9.7 %collective-permute-start.37 = (bf16[2,96,768]{2,1,0:T(8,128)(2,1)S(1)}, bf16[2,96,768]{2,1,0:T(8,128)(2,1)S(1)}, u32[]{:S(2)}, u32[]{:S(2)}) collective-permute-start(bf16[2,96,768]{2,1,0:T(8,128)(2,1)S(1)} %fusion.29), channel_id=1, source_target_pairs={{0,2},{1,3},{2,0},{3,1},{4,6},{5,7},{6,4},{7,5},{8,10},{9,11},{10,... | collective-permute-start | bytes 884744 | tf_op jit(solution)/shard_map/ppermute | solution.py:141
  545.3 7.2 %collective-permute-start.23 = (bf16[72,768]{1,0:T(8,128)(2,1)S(1)}, bf16[72,768]{1,0:T(8,128)(2,1)S(1)}, u32[]{:S(2)}, u32[]{:S(2)}) collective-permute-start(bf16[72,768]{1,0:T(8,128)(2,1)S(1)} %fusion.42), channel_id=1, source_target_pairs={{0,1},{1,0},{2,3},{3,2},{4,5},{5,4},{6,7},{7,6},{8,9},{9,8},{10,11... | collective-permute-start | bytes 331784 | tf_op jit(solution)/shard_map/ppermute | solution.py:141
  547.4 8.6 %collective-permute-start.32 = (bf16[2,96,768]{2,1,0:T(8,128)(2,1)S(1)}, bf16[2,96,768]{2,1,0:T(8,128)(2,1)S(1)}, u32[]{:S(2)}, u32[]{:S(2)}) collective-permute-start(bf16[2,96,768]{2,1,0:T(8,128)(2,1)S(1)} %fusion.30), channel_id=1, source_target_pairs={{0,16},{8,24},{16,0},{24,8},{1,17},{9,25},{17,1},{25,9},{2,18},{10... | collective-permute-start | bytes 884744 | tf_op jit(solution)/shard_map/ppermute | solution.py:141
  551.6 5.9 %collective-permute-start.38 = (bf16[96,768]{1,0:T(8,128)(2,1)S(1)}, bf16[96,768]{1,0:T(8,128)(2,1)S(1)}, u32[]{:S(2)}, u32[]{:S(2)}) collective-permute-start(bf16[96,768]{1,0:T(8,128)(2,1)S(1)} %fusion.36), channel_id=1, source_target_pairs={{0,1},{1,0},{2,3},{3,2},{4,5},{5,4},{6,7},{7,6},{8,9},{9,8},{10,11... | collective-permute-start | bytes 442376 | tf_op jit(solution)/shard_map/ppermute | solution.py:141
  557.1 8.3 %collective-permute-start.33 = (bf16[96,768]{1,0:T(8,128)(2,1)S(1)}, bf16[96,768]{1,0:T(8,128)(2,1)S(1)}, u32[]{:S(2)}, u32[]{:S(2)}) collective-permute-start(bf16[96,768]{1,0:T(8,128)(2,1)S(1)} %fusion.38), channel_id=1, source_target_pairs={{0,4},{1,5},{2,6},{3,7},{4,0},{5,1},{6,2},{7,3},{8,12},{9,13},{10,... | collective-permute-start | bytes 442376 | tf_op jit(solution)/shard_map/ppermute | solution.py:141
  (44 other events, 299.2 us)

commit v2 on v1

--- a/solution.py
+++ b/solution.py
@@ -1,9 +1,11 @@
+import functools
+
 import jax
 import jax.numpy as jnp
 from jax import lax
+from jax.experimental import pallas as pl
+from jax.experimental.pallas import tpu as pltpu
 from jax.sharding import PartitionSpec as P
-
-HEADS = 12
 
 
 highest = lax.Precision.HIGHEST
@@ -33,107 +35,202 @@
     return wave_rows + jax.nn.gelu(jnp.dot(wave_rows, weight, precision=highest))
 
 
-def score_block(query_heads, key_heads, seg_rows, seg_all, score_scale):
-    scores = (
-        jnp.einsum("qhd,khd->hqk", query_heads, key_heads, preferred_element_type=jnp.float32)
-        * score_scale
-    )
-    same_segment = seg_rows[:, None] == seg_all[None, :]
-    return jnp.where(same_segment[None], scores, -1000000000.0)
-
-
-def attend_forward(queries, keys, values, segment, head_count):
-    length, model_width = queries.shape
-    head_size = model_width // head_count
-    score_scale = head_size ** (-0.5)
-    block_rows = min(512, length)
-    query_heads = queries.reshape(length, head_count, head_size)
-    key_heads = keys.reshape(length, head_count, head_size)
-    value_heads = values.reshape(length, head_count, head_size)
-    outputs = []
-    totals = []
-    for first_row in range(0, length, block_rows):
-        rows_end = first_row + block_rows
-        scores = score_block(
-            query_heads[first_row:rows_end],
-            key_heads,
-            segment[first_row:rows_end],
-            segment,
-            score_scale,
-        )
-        row_peak = jnp.max(scores, axis=-1, keepdims=True)
-        log_total = row_peak + jnp.log(jnp.sum(jnp.exp(scores - row_peak), axis=-1, keepdims=True))
-        weights_low = jnp.exp(scores - log_total).astype(jnp.bfloat16)
-        mixed_rows = jnp.einsum(
-            "hqk,khd->qhd", weights_low, value_heads, preferred_element_type=jnp.float32
-        )
-        outputs.append(mixed_rows.reshape(-1, model_width))
-        totals.append(log_total)
-    return (jnp.concatenate(outputs, axis=0).astype(jnp.bfloat16), jnp.concatenate(totals, axis=1))
-
-
-def attend_back(queries, keys, values, segment, totals, grad_mixed, head_count):
-    length, model_width = queries.shape
-    head_size = model_width // head_count
-    score_scale = head_size ** (-0.5)
-    block_rows = min(512, length)
-    query_heads = queries.reshape(length, head_count, head_size)
-    key_heads = keys.reshape(length, head_count, head_size)
-    value_heads = values.reshape(length, head_count, head_size)
-    grad_heads = grad_mixed.reshape(length, head_count, head_size)
-    grad_keys = jnp.zeros((length, head_count, head_size), jnp.float32)
-    grad_values = jnp.zeros((length, head_count, head_size), jnp.float32)
-    grad_queries = []
-    for first_row in range(0, length, block_rows):
-        rows_end = first_row + block_rows
-        scores = score_block(
-            query_heads[first_row:rows_end],
-            key_heads,
-            segment[first_row:rows_end],
-            segment,
-            score_scale,
-        )
-        weights = jnp.exp(scores - totals[:, first_row:rows_end])
-        weights_low = weights.astype(jnp.bfloat16)
-        grad_weights = jnp.einsum(
-            "qhd,khd->hqk",
-            grad_heads[first_row:rows_end],
-            value_heads,
-            preferred_element_type=jnp.float32,
-        )
-        grad_scores = (
-            weights * (grad_weights - jnp.sum(weights * grad_weights, axis=-1, keepdims=True))
-        ).astype(jnp.bfloat16)
-        grad_queries.append(
-            jnp.einsum(
-                "hqk,khd->qhd", grad_scores, key_heads, preferred_element_type=jnp.float32
-            ).reshape(-1, model_width)
-            * score_scale
-        )
-        grad_keys = (
-            grad_keys
-            + jnp.einsum(
-                "hqk,qhd->khd",
-                grad_scores,
-                query_heads[first_row:rows_end],
-                preferred_element_type=jnp.float32,
-            )
-            * score_scale
-        )
-        grad_values = grad_values + jnp.einsum(
-            "hqk,qhd->khd",
-            weights_low,
-            grad_heads[first_row:rows_end],
-            preferred_element_type=jnp.float32,
-        )
-    return jnp.concatenate(
-        [
-            jnp.concatenate(grad_queries, axis=0),
-            grad_keys.reshape(length, model_width),
-            grad_values.reshape(length, model_width),
+BLOCK = 256
+STEP = 128
+FAR = 2.0**30
+LANES = (((1,), (1,)), ((), ()))
+ROWS = (((0,), (0,)), ((), ()))
+
+
+def dot32(left, right, dims):
+    return lax.dot_general(left, right, dims, preferred_element_type=jnp.float32)
+
+
+def windows(segment_ids):
+    length = segment_ids.shape[1]
+    first = segment_ids[:, ::BLOCK]
+    last = segment_ids[:, BLOCK - 1 :: BLOCK]
+    begin = jnp.sum(segment_ids[:, None, :] < first[:, :, None], axis=-1)
+    end = jnp.sum(segment_ids[:, None, :] <= last[:, :, None], axis=-1)
+    low = begin // STEP
+    count = (end + STEP - 1) // STEP - low
+    return jnp.stack([low, count - 1], axis=-1).astype(jnp.int32).reshape(-1)
+
+
+def features(segment_ids):
+    lane = jnp.arange(128, dtype=jnp.int32)
+    code = segment_ids.reshape(-1, 1)
+    same = (code == (lane % 64)[None, :])
+    used = (lane % 64 < 4)[None, :]
+    query_side = jnp.where(same & used, 1.0, 0.0)
+    key_side = jnp.where(used & ~same, -FAR, 0.0)
+    return query_side.astype(jnp.bfloat16), key_side.astype(jnp.bfloat16)
+
+
+def head_masks():
+    lane = lax.broadcasted_iota(jnp.int32, (1, 128), 1)
+    low = jnp.where(lane < 64, 1.0, 0.0)
+    return low.astype(jnp.bfloat16), (1.0 - low).astype(jnp.bfloat16)
+
+
+def forward_kernel(win, q_ref, k_ref, v_ref, qf_ref, kf_ref, o_ref, lse_ref, qa, ka, va):
+    length = q_ref.shape[0]
+    blocks = length // BLOCK
+    base = pl.program_id(0) * blocks * 2
+    for h, mask in enumerate(head_masks()):
+        other = jnp.bfloat16(1.0) - mask
+        qa[h] = q_ref[...] * (mask * jnp.bfloat16(0.125)) + qf_ref[...] * other
+        ka[h] = k_ref[...] * mask + kf_ref[...] * other
+        va[h] = v_ref[...] * mask + other
+
+    def one_block(block, carry):
+        rows = pl.ds(pl.multiple_of(block * BLOCK, BLOCK), BLOCK)
+        low = pl.multiple_of(win[base + 2 * block] * STEP, STEP)
+
+        def run(width):
+            keys = pl.ds(low, width)
+            mixes, peaks = [], []
+            for h in range(2):
+                scores = dot32(qa[h, rows, :], ka[h, keys, :], LANES)
+                peak = jnp.max(scores, axis=1, keepdims=True)
+                probs = jnp.exp(scores - peak).astype(jnp.bfloat16)
+                mixes.append(jnp.dot(probs, va[h, keys, :], preferred_element_type=jnp.float32))
+                peaks.append(peak)
+            low_lanes = lax.broadcasted_iota(jnp.int32, (1, 128), 1) < 64
+            mixed = jnp.where(low_lanes, mixes[0], mixes[1])
+            total = pltpu.roll(jnp.where(low_lanes, mixes[1], mixes[0]), 64, 1)
+            o_ref[rows, :] = (mixed / total).astype(jnp.bfloat16)
+            both = (jnp.where(low_lanes, peaks[0], peaks[1]) + jnp.log(total)).T
+            lse_ref[0, 0, 0:1, rows] = both[0:1]
+            lse_ref[0, 0, 1:2, rows] = both[64:65]
+
+        count = win[base + 2 * block + 1]
+        for size in range(length // STEP):
+            pl.when(count == size)(functools.partial(run, (size + 1) * STEP))
+        return carry
+
+    lax.fori_loop(0, blocks, one_block, 0)
+
+
+def back_kernel(win, q_ref, k_ref, v_ref, qf_ref, kf_ref, g_ref, o_ref, lse_ref, out_ref, qa, ka, qh, kh, vh, gh, delta, dk, dv):
+    length = q_ref.shape[0]
+    blocks = length // BLOCK
+    base = pl.program_id(0) * blocks * 2
+    masks = head_masks()
+    for h, mask in enumerate(masks):
+        other = jnp.bfloat16(1.0) - mask
+        scaled = q_ref[...] * (mask * jnp.bfloat16(0.125))
+        qh[h] = scaled
+        qa[h] = scaled + qf_ref[...] * other
+        own = k_ref[...] * mask
+        kh[h] = own
+        ka[h] = own + kf_ref[...] * other
+        vh[h] = v_ref[...] * mask
+        gh[h] = g_ref[...] * mask
+    product = g_ref[...].astype(jnp.float32) * o_ref[...].astype(jnp.float32)
+    turned = product.T
+    delta[0:1, :] = jnp.sum(turned[:64], axis=0, keepdims=True)
+    delta[1:2, :] = jnp.sum(turned[64:], axis=0, keepdims=True)
+    dk[...] = jnp.zeros_like(dk)
+    dv[...] = jnp.zeros_like(dv)
+
+    def one_block(block, carry):
+        rows = pl.ds(pl.multiple_of(block * BLOCK, BLOCK), BLOCK)
+        low = pl.multiple_of(win[base + 2 * block] * STEP, STEP)
+
+        def run(width):
+            keys = pl.ds(low, width)
+            turned_grad = None
+            for h in range(2):
+                scores = dot32(ka[h, keys, :], qa[h, rows, :], LANES)
+                probs = jnp.exp(scores - lse_ref[0, 0, h : h + 1, rows])
+                grad_probs = dot32(vh[h, keys, :], gh[h, rows, :], LANES)
+                grad_scores = (probs * (grad_probs - delta[h : h + 1, rows])).astype(jnp.bfloat16)
+                dv[keys, :] += jnp.dot(probs.astype(jnp.bfloat16), gh[h, rows, :], preferred_element_type=jnp.float32)
+                dk[keys, :] += jnp.dot(grad_scores, qh[h, rows, :], preferred_element_type=jnp.float32)
+                term = dot32(grad_scores, kh[h, keys, :], ROWS)
+                turned_grad = term if h == 0 else turned_grad + term
+            out_ref[0, rows, :] = (turned_grad * 0.125).astype(jnp.bfloat16)
+
+        count = win[base + 2 * block + 1]
+        for size in range(length // STEP):
+            pl.when(count == size)(functools.partial(run, (size + 1) * STEP))
+        return carry
+
+    lax.fori_loop(0, blocks, one_block, 0)
+    out_ref[1] = dk[...].astype(jnp.bfloat16)
+    out_ref[2] = dv[...].astype(jnp.bfloat16)
+
+
+def attend_forward(projected, segment_ids, win, query_side, key_side):
+    seqs, length = segment_ids.shape
+    width = projected.shape[1] // 3
+    pairs = width // 128
+
+    def columns(offset):
+        return pl.BlockSpec((length, 128), lambda s, p, w: (s, p + offset))
+
+    fixed = pl.BlockSpec((length, 128), lambda s, p, w: (s, 0))
+    return pl.pallas_call(
+        forward_kernel,
+        grid_spec=pltpu.PrefetchScalarGridSpec(
+            num_scalar_prefetch=1,
+            grid=(seqs, pairs),
+            in_specs=[columns(0), columns(pairs), columns(2 * pairs), fixed, fixed],
+            out_specs=[
+                columns(0),
+                pl.BlockSpec((1, 1, 8, length), lambda s, p, w: (s, p, 0, 0)),
+            ],
+            scratch_shapes=[pltpu.VMEM((2, length, 128), jnp.bfloat16)] * 3,
+        ),
+        out_shape=[
+            jax.ShapeDtypeStruct((seqs * length, width), jnp.bfloat16),
+            jax.ShapeDtypeStruct((seqs, pairs, 8, length), jnp.float32),
         ],
-        axis=1,
-    )
+        compiler_params=pltpu.CompilerParams(vmem_limit_bytes=48 << 20),
+        cost_estimate=pl.CostEstimate(flops=4 * seqs * length * length * width, bytes_accessed=8 * seqs * length * width, transcendentals=0),
+        name="attend_forward",
+    )(win, projected, projected, projected, query_side, key_side)
+
+
+def attend_back(projected, segment_ids, win, query_side, key_side, grad, mixed, lse):
+    seqs, length = segment_ids.shape
+    width = projected.shape[1] // 3
+    pairs = width // 128
+
+    def columns(offset):
+        return pl.BlockSpec((length, 128), lambda s, p, w: (s, p + offset))
+
+    fixed = pl.BlockSpec((length, 128), lambda s, p, w: (s, 0))
+    low = pltpu.VMEM((2, length, 128), jnp.bfloat16)
+    return pl.pallas_call(
+        back_kernel,
+        grid_spec=pltpu.PrefetchScalarGridSpec(
+            num_scalar_prefetch=1,
+            grid=(seqs, pairs),
+            in_specs=[
+                columns(0),
+                columns(pairs),
+                columns(2 * pairs),
+                fixed,
+                fixed,
+                columns(0),
+                columns(0),
+                pl.BlockSpec((1, 1, 8, length), lambda s, p, w: (s, p, 0, 0)),
+            ],
+            out_specs=pl.BlockSpec((3, length, 128), lambda s, p, w: (0, s, p)),
+            scratch_shapes=[low] * 6
+            + [
+                pltpu.VMEM((8, length), jnp.float32),
+                pltpu.VMEM((length, 128), jnp.float32),
+                pltpu.VMEM((length, 128), jnp.float32),
+            ],
+        ),
+        out_shape=jax.ShapeDtypeStruct((3, seqs * length, width), jnp.bfloat16),
+        compiler_params=pltpu.CompilerParams(vmem_limit_bytes=48 << 20),
+        cost_estimate=pl.CostEstimate(flops=10 * seqs * length * length * width, bytes_accessed=14 * seqs * length * width, transcendentals=0),
+        name="attend_back",
+    )(win, projected, projected, projected, query_side, key_side, grad, mixed, lse)
 
 
 def swap(piece, axis, mask):
@@ -224,8 +321,6 @@
     model_width = qkv_weight.shape[0]
     patch_pixels = pixels.shape[2]
     wave_count = wave_table.shape[0]
-    seq_count = segment_ids.shape[0]
-    length = segment_ids.shape[1]
     sensors = sensor_table.shape[0]
     code_width = wave_table.shape[1]
     part_rows = slots_dev * patch_pixels
@@ -280,15 +375,9 @@
     projected = jnp.dot(normed1_low, qkv_weight, preferred_element_type=jnp.float32).astype(
         jnp.bfloat16
     )
-    queries = projected[:, :model_width].reshape(seq_count, length, model_width)
-    keys = projected[:, model_width : 2 * model_width].reshape(seq_count, length, model_width)
-    values = projected[:, 2 * model_width :].reshape(seq_count, length, model_width)
-
-    def forward_one(packed):
-        return attend_forward(packed[0], packed[1], packed[2], packed[3], HEADS)
-
-    attended, totals = lax.map(forward_one, (queries, keys, values, segment_ids))
-    attended = attended.reshape(tok_dev, model_width)
+    window = windows(segment_ids)
+    query_side, key_side = features(segment_ids)
+    attended, totals = attend_forward(projected, segment_ids, window, query_side, key_side)
     after = start_rows + jnp.dot(attended, proj_weight, preferred_element_type=jnp.float32)
     normed2, unit2, inverse2 = layer_norm(after, ln2_gain)
     normed2_low = normed2.astype(jnp.bfloat16)
@@ -313,25 +402,19 @@
         jnp.bfloat16
     )
 
-    def back_one(packed):
-        return attend_back(packed[0], packed[1], packed[2], packed[3], packed[4], packed[5], HEADS)
-
-    grad_projected = lax.map(
-        back_one,
-        (
-            queries,
-            keys,
-            values,
-            segment_ids,
-            totals,
-            grad_attended.reshape(seq_count, length, model_width),
-        ),
-    )
-    grad_projected = grad_projected.reshape(tok_dev, 3 * model_width).astype(jnp.bfloat16)
-    qkv_term = jnp.dot(grad_projected.T, normed1_low, preferred_element_type=jnp.float32).astype(
-        jnp.bfloat16
-    )
-    grad_normed1 = jnp.dot(grad_projected, qkv_weight.T, preferred_element_type=jnp.float32)
+    grad_projected = attend_back(
+        projected, segment_ids, window, query_side, key_side, grad_attended, attended, totals
+    )
+    qkv_term = lax.dot_general(
+        grad_projected, normed1_low, (((1,), (0,)), ((), ())), preferred_element_type=jnp.float32
+    )
+    qkv_term = qkv_term.astype(jnp.bfloat16).reshape(-1, model_width)
+    grad_normed1 = lax.dot_general(
+        grad_projected,
+        qkv_weight.reshape(model_width, 3, model_width),
+        (((0, 2), (1, 2)), ((), ())),
+        preferred_element_type=jnp.float32,
+    )
     grad_start_norm, ln1_term = norm_back(grad_normed1, unit1, inverse1, ln1_gain)
     grad_start = grad_after + grad_start_norm
     sensor_term = jnp.sum(grad_start, axis=0)

time: 572 us -> 405 us (0.71)
  matrix products: 260 us -> 112 us
  other arithmetic: 109 us -> 41.4 us
  Pallas kernels: 0 us -> 67.5 us
  local copies, waits for them, and re-layouts: 51.8 us -> 33.5 us
    dot_general x14 -> x2, matrix products: 155 us -> 15.1 us  [the longest x1 7.84 us: shards(): lax.dot_general(grad_projected, qkv_weight.reshape(model_width, 3, model_...]
    pallas_call x0 -> x2, Pallas kernels: none -> 67.5 us  [the longest x1 36.7 us: attend_back(): pl.pallas_call(back_kernel, grid_spec=pltpu.PrefetchScalarGridSpec(num_sc...]
    convert_element_type x1, other arithmetic: 43.1 us -> 0.93 us  [features(): return (query_side.astype(jnp.bfloat16), key_side.astype(jnp.bfloat16))]
    reduce_sum x2 -> x1, other arithmetic: 24 us -> 0.22 us  [windows(): begin = jnp.sum(segment_ids[:, None, :] < first[:, :, None], axis=-1)]
    slice x8 -> x2, local copies, waits for them, and re-layouts: 14 us -> 0.19 us  [the longest x1 0.09 us: windows(): last = segment_ids[:, BLOCK - 1::BLOCK]]
    unnamed x123 -> x84, local copies, waits for them, and re-layouts: 8.58 us -> 12.5 us
  transfers between devices with their start and end apart: 39 -> 39, of which waited for: 20 -> 20; matrix products, arithmetic and copies ran while one was open for 15% -> 19% of each run, Pallas kernels for 0% -> 0%
where the time goes in v2:
time: 405 us; the launch traced here: 401 us
  matrix products  112 us (28%)
  waiting for transfers between devices  104 us (26%)
  Pallas kernels  67.5 us (17%)
  other arithmetic  41.4 us (10%)
  starting transfers between devices  40.7 us (10%)
  local copies, waits for them, and re-layouts  33.5 us (8%)
    ppermute x39, waiting for transfers between devices, swap(): return lax.ppermute(piece, axis, [(i, i ^ mask) for i in range(count)])  104 us
    ppermute x39, starting transfers between devices, swap(): return lax.ppermute(piece, axis, [(i, i ^ mask) for i in range(count)])  40.7 us
    pallas_call x1, Pallas kernels, attend_back(): pl.pallas_call(back_kernel, grid_spec=pltpu.PrefetchScalarGridSpec(num_sc...  36.7 us
    pallas_call x1, Pallas kernels, attend_forward(): pl.pallas_call(forward_kernel, grid_spec=pltpu.PrefetchScalarGridSpec(num...  30.8 us
    convert_element_type x16, other arithmetic, scatter_sum(): send = sum((lax.dynamic_index_in_dim(part, 1 - mine, dim, False).astype(j...  20.5 us
    dot_general x1, matrix products, shards(): jnp.dot(out_grad, fc2_weight.T, preferred_element_type=jnp.float32)  15.3 us
    unnamed x84, local copies, waits for them, and re-layouts  12.5 us
    dot_general x1, matrix products, shards(): jnp.dot(act_low, fc2_weight, preferred_element_type=jnp.float32)  12.1 us
  transfers between devices with their start and end apart: 39, of which 20 were waited for; matrix products, arithmetic and copies ran while one was open for 19% of the time, Pallas kernels for 0%

profile of v2, /device:TPU:0, one launch (start us, length us, event | category | flops | bytes accessed | tf_op | source)
XLA Modules:
  0.0 401.2 jit_solution(3363181106484649535)
XLA Ops:
  1.8 2.2 constant_dynamic-slice_fusion.33
  4.5 2.5 collective-permute-start.1
  11.5 6.4 %fusion = bf16[8,49152]{1,0:T(8,128)(2,1)S(1)} fusion(bf16[128,49152]{1,0:T(8,128)(2,1)} %param.23, bf16[8]{0:T(256)(128)(2,1)S(1)} %get-tuple-element.108, f32[8,128]{1,0:T(8,128)S(1)} %fusion.87, bf16[128,128]{1,0:T(8,128)(2,1)S(1)} %copy-done.11), kind=kOutput, calls=%fused_computation.1 | convolution fusion | flops 102902784 | bytes 13406224 | tf_op jit(solution)/shard_map/dot_general | solution.py:362
  21.5 5.8 %copy.95 = bf16[768,2304]{0,1:T(8,128)(2,1)} copy(bf16[768,2304]{1,0:T(8,128)(2,1)} %param.26) | data formatting | bytes 7077888 | tf_op args[10]
  31.2 2.2 collective-permute-done.7
  34.6 2.6 collective-permute-start.8
  37.2 2.2 collective-permute-done.8
  48.7 2.6 add_reduce_fusion
  52.1 5.7 %convolution_convert_fusion.1.q_ref.k_ref.v_ref = bf16[1024,2304]{1,0:T(8,128)(2,1)} fusion(bf16[768,2304]{1,0:T(8,128)(2,1)S(1)} %copy-done.1, f32[768]{0:T(1024)S(1)} %copy-done.18, f32[1024,768]{0,1:T(8,128)S(1)} %get-tuple-element.112, f32[1024]{0:T(1024)S(1)} %add_rsqrt_fusion.1, f32[1024]{0:T(1024)S(1)} %broadcast_multiply_fusion.5, ...), kind=kOutput, calls=%fused_computation.12 | convolution fusion | flops 3630170112 | bytes 11417600 | tf_op jit(solution)/shard_map/dot_general | solution.py:375
  57.8 30.8 %attend_forward.1 = (bf16[1024,768]{1,0:T(8,128)(2,1)S(1)}, f32[1,6,8,1024]{3,2,1,0:T(8,128)S(1)}) custom-call(s32[8]{0:T(128)S(1)} %reshape.755.win, bf16[1024,2304]{1,0:T(8,128)(2,1)} %convolution_convert_fusion.1.q_ref.k_ref.v_ref, bf16[1024,2304]{1,0:T(8,128)(2,1)} %convolution_convert_fusion.1.q_ref.k_ref.v_ref, ...), custom_call_target="tpu_custom_call" | custom-call | flops 3221225472 | bytes 6291456 | tf_op jit(solution)/shard_map/attend_forward/pallas_call | solution.py:174
  91.1 8.2 %fusion.117 = f32[1024,3072]{1,0:T(8,128)} fusion(bf16[768,3072]{1,0:T(8,128)(2,1)S(1)} %bitcast.423, f32[1024,768]{0,1:T(8,128)S(1)} %get-tuple-element.114, f32[768]{0:T(1024)S(1)} %copy-done.10, f32[1024]{0:T(1024)S(1)} %add_rsqrt_fusion, f32[1024]{0:T(1024)S(1)} %broadcast_multiply_fusion.4), kind=kOutput, calls=%fused_computation.319 | convolution fusion | flops 4834983936 | bytes 20458496 | tf_op jit(solution)/shard_map/dot_general | solution.py:384
  99.3 11.7 %convolution_convert_fusion.2 = bf16[3072,768]{1,0:T(8,128)(2,1)} fusion(bf16[1024,768]{1,0:T(8,128)(2,1)S(1)} %copy-done.6, f32[1024,3072]{1,0:T(8,128)} %fusion.117), kind=kOutput, calls=%fused_computation.13 | convolution fusion | flops 4862509056 | bytes 18874368 | tf_op jit(solution)/shard_map/dot_general | solution.py:388
  111.1 15.3 %fusion.7 = bf16[1024,3072]{1,0:T(8,128)(2,1)} fusion(f32[1024,3072]{1,0:T(8,128)} %fusion.117, bf16[1024,768]{1,0:T(8,128)(2,1)S(1)} %copy-done.6, bf16[3072,768]{1,0:T(8,128)(2,1)} %param.30), kind=kOutput, calls=%fused_computation.10 | convolution fusion | flops 4894752768 | bytes 25165824 | tf_op jit(solution)/shard_map/dot_general | solution.py:387
  126.4 10.7 %convolution_convert_fusion.3 = bf16[3072,768]{1,0:T(8,128)(2,1)} fusion(bf16[1024,3072]{1,0:T(8,128)(2,1)} %fusion.7, f32[1024,768]{0,1:T(8,128)S(1)} %get-tuple-element.114, f32[768]{0:T(1024)S(1)} %copy-done.10, f32[1024]{0:T(1024)S(1)} %add_rsqrt_fusion, f32[1024]{0:T(1024)S(1)} %broadcast_multiply_fusion.4), kind=kOutput, calls=%fused_computation.14 | convolution fusion | flops 4837343232 | bytes 14167040 | tf_op jit(solution)/shard_map/dot_general | solution.py:391
  137.1 5.5 %multiply_reduce_fusion = (f32[768]{0:T(1024)S(1)}, f32[1024]{0:T(1024)S(1)}, f32[1024]{0:T(1024)S(1)}, f32[1024,768]{0,1:T(8,128)S(1)}) fusion(f32[1024,768]{0,1:T(8,128)S(1)} %get-tuple-element.114, f32[1024]{0:T(1024)S(1)} %add_rsqrt_fusion, f32[1024]{0:T(1024)S(1)} %broadcast_multiply_fusion.4, f32[768]{0:T(1024)S(1)} %copy-done.10, ...), kind=kOutput, calls=%fused_computation.18 | convolution fusion | flops 4838126592 | bytes 17324032 | tf_op jit(solution)/shard_map/dot_general | solution.py:394
  143.7 2.4 convolution_convert_fusion.6
  147.5 36.7 %attend_back.1 = bf16[3,1024,768]{2,1,0:T(8,128)(2,1)} custom-call(s32[8]{0:T(128)S(1)} %reshape.755.win, bf16[1024,2304]{1,0:T(8,128)(2,1)} %convolution_convert_fusion.1.q_ref.k_ref.v_ref, bf16[1024,2304]{1,0:T(8,128)(2,1)} %convolution_convert_fusion.1.q_ref.k_ref.v_ref, bf16[1024,2304]{1,0:T(8,128)(2,1)} %convolution_convert_fusion.1.q_ref.k_ref.v_ref, ...), custom_call_target="tpu_custom_call" | custom-call | flops 8053063680 | bytes 11010048 | tf_op jit(solution)/shard_map/attend_back/pallas_call | solution.py:206
  184.3 7.3 %convolution_convert_fusion.4 = bf16[3,768,768]{2,1,0:T(8,128)(2,1)S(1)} fusion(bf16[3,1024,768]{2,1,0:T(8,128)(2,1)} %attend_back.1, f32[768]{0:T(1024)S(1)} %copy-done.18, f32[1024,768]{0,1:T(8,128)S(1)} %get-tuple-element.112, f32[1024]{0:T(1024)S(1)} %add_rsqrt_fusion.1, f32[1024]{0:T(1024)S(1)} %broadcast_multiply_fusion.5, ...), kind=kOutput, calls=%fused_computation.35 | convolution fusion | flops 3629580288 | bytes 11417600 | tf_op jit(solution)/shard_map/dot_general | solution.py:408
  191.6 7.8 %fusion.8 = (f32[768]{0:T(1024)S(1)}, f32[1024]{0:T(1024)S(1)}, f32[1024]{0:T(1024)S(1)}, f32[1024,768,1]{0,1,2:T(8,128)S(1)}) fusion(f32[1024]{0:T(1024)S(1)} %add_rsqrt_fusion.1, f32[1024]{0:T(1024)S(1)} %broadcast_multiply_fusion.5, f32[1024,768]{0,1:T(8,128)S(1)} %get-tuple-element.112, f32[768]{0:T(1024)S(1)} %convolution_reduce_fusion, ...), kind=kOutput, calls=%fused_computation.17 | convolution fusion | flops 3630953728 | bytes 14574592 | tf_op jit(solution)/shard_map/dot_general | solution.py:412
  199.4 2.0 fusion.118
  201.4 2.3 convolution_convert_fusion.7
  204.8 12.1 %convolution_add_fusion = f32[1024,768]{0,1:T(8,128)} fusion(f32[1024,768]{0,1:T(8,128)S(1)} %get-tuple-element.114, bf16[3072,768]{1,0:T(8,128)(2,1)} %param.30, f32[1024,3072]{1,0:T(8,128)} %fusion.117), kind=kOutput, calls=%fused_computation.45 | convolution fusion | flops 4860936192 | bytes 23592960 | tf_op jit(solution)/shard_map/dot_general | solution.py:386
  216.9 3.2 dynamic-slice_bitcast_fusion
  225.8 3.1 collective-permute-start.4
  230.0 3.8 copy.112
  239.7 4.4 %collective-permute-done.5 = bf16[128,1024]{1,0:T(8,128)(2,1)S(1)} collective-permute-done((bf16[128,1024]{1,0:T(8,128)(2,1)S(1)}, bf16[128,1024]{1,0:T(8,128)(2,1)S(1)}, u32[]{:S(2)}, u32[]{:S(2)}) %collective-permute-start.5) | collective-permute-done | bytes 262176 | tf_op jit(solution)/shard_map/ppermute | solution.py:238
  245.5 2.3 fusion.29
  248.4 3.4 collective-permute-done.10
  253.3 2.9 fusion.18
  258.1 3.1 collective-permute-done.12
  261.3 3.7 collective-permute-done.13
  265.8 3.1 collective-permute-done.14
  269.0 4.6 %collective-permute-done.16 = bf16[4,1,8,1536]{3,2,0,1:T(8,128)(2,1)S(1)} collective-permute-done((bf16[4,1,8,1536]{3,2,0,1:T(8,128)(2,1)S(1)}, bf16[4,1,8,1536]{3,2,0,1:T(8,128)(2,1)S(1)}, u32[]{:S(2)}, u32[]{:S(2)}) %collective-permute-start.16) | collective-permute-done | bytes 98336 | tf_op jit(solution)/shard_map/ppermute | solution.py:238
  273.6 2.8 collective-permute-start.15
  276.4 2.6 collective-permute-done.15
  283.8 2.6 collective-permute-start.18
  291.4 2.3 collective-permute-start.35
  296.8 2.5 collective-permute-start.30
  299.3 32.4 %collective-permute-done.20 = bf16[2,2,2,72,768]{4,3,2,1,0:T(8,128)(2,1)S(1)} collective-permute-done((bf16[2,2,2,72,768]{4,3,2,1,0:T(8,128)(2,1)S(1)}, bf16[2,2,2,72,768]{4,3,2,1,0:T(8,128)(2,1)S(1)}, u32[]{:S(2)}, u32[]{:S(2)}) %collective-permute-start.20) | collective-permute-done | bytes 884768 | tf_op jit(solution)/shard_map/ppermute | solution.py:238
  332.9 2.8 collective-permute-start.21
  343.0 9.2 %collective-permute-done.27 = bf16[2,24,768]{2,1,0:T(8,128)(2,1)S(1)} collective-permute-done((bf16[2,24,768]{2,1,0:T(8,128)(2,1)S(1)}, bf16[2,24,768]{2,1,0:T(8,128)(2,1)S(1)}, u32[]{:S(2)}, u32[]{:S(2)}) %collective-permute-start.27) | collective-permute-done | bytes 73760 | tf_op jit(solution)/shard_map/ppermute | solution.py:238
  353.0 2.7 collective-permute-start.28
  355.7 5.0 %collective-permute-done.21 = bf16[2,2,72,768]{3,2,1,0:T(8,128)(2,1)S(1)} collective-permute-done((bf16[2,2,72,768]{3,2,1,0:T(8,128)(2,1)S(1)}, bf16[2,2,72,768]{3,2,1,0:T(8,128)(2,1)S(1)}, u32[]{:S(2)}, u32[]{:S(2)}) %collective-permute-start.21) | collective-permute-done | bytes 442400 | tf_op jit(solution)/shard_map/ppermute | solution.py:238
  362.7 10.6 %collective-permute-done.36 = bf16[2,2,96,768]{3,2,1,0:T(8,128)(2,1)S(1)} collective-permute-done((bf16[2,2,96,768]{3,2,1,0:T(8,128)(2,1)S(1)}, bf16[2,2,96,768]{3,2,1,0:T(8,128)(2,1)S(1)}, u32[]{:S(2)}, u32[]{:S(2)}) %collective-permute-start.36) | collective-permute-done | bytes 589856 | tf_op jit(solution)/shard_map/ppermute | solution.py:238
  376.1 1.9 collective-permute-done.22
  380.3 3.9 collective-permute-done.37
  387.1 2.0 collective-permute-done.32
  392.8 6.3 %collective-permute-done.33 = bf16[96,768]{1,0:T(8,128)(2,1)S(1)} collective-permute-done((bf16[96,768]{1,0:T(8,128)(2,1)S(1)}, bf16[96,768]{1,0:T(8,128)(2,1)S(1)}, u32[]{:S(2)}, u32[]{:S(2)}) %collective-permute-start.33) | collective-permute-done | bytes 147488 | tf_op jit(solution)/shard_map/ppermute | solution.py:238
  (236 shorter events, 86.3 us)
Async XLA Ops:
  0.6 88.0 %copy-start = (bf16[768,768]{1,0:T(8,128)(2,1)S(1)}, bf16[768,768]{1,0:T(8,128)(2,1)}, u32[]{:S(2)}) copy-start(bf16[768,768]{1,0:T(8,128)(2,1)} %param.27) | copy-start | bytes 3538948
  4.0 40.7 %collective-permute-start = (bf16[128,1024]{1,0:T(8,128)(2,1)}, bf16[128,1024]{1,0:T(8,128)(2,1)}, u32[]{:S(2)}, u32[]{:S(2)}) collective-permute-start(bf16[128,1024]{1,0:T(8,128)(2,1)} %get-tuple-element.79), channel_id=1, source_target_pairs={{0,8},{8,0},{16,24},{24,16},{1,9},{9,1},{17,25},{25,17},{2,10},{10... | collective-permute-start | bytes 786440 | tf_op jit(solution)/shard_map/ppermute | solution.py:238
  4.5 41.9 %collective-permute-start.1 = (bf16[128,1024]{1,0:T(8,128)(2,1)}, bf16[128,1024]{1,0:T(8,128)(2,1)}, u32[]{:S(2)}, u32[]{:S(2)}) collective-permute-start(bf16[128,1024]{1,0:T(8,128)(2,1)} %get-tuple-element.78), channel_id=1, source_target_pairs={{0,16},{8,24},{16,0},{24,8},{1,17},{9,25},{17,1},{25,9},{2,18},{10... | collective-permute-start | bytes 786440 | tf_op jit(solution)/shard_map/ppermute | solution.py:238
  6.9 41.1 %collective-permute-start.2 = (bf16[128,1024]{1,0:T(8,128)(2,1)}, bf16[128,1024]{1,0:T(8,128)(2,1)S(1)}, u32[]{:S(2)}, u32[]{:S(2)}) collective-permute-start(bf16[128,1024]{1,0:T(8,128)(2,1)} %get-tuple-element.77), channel_id=1, source_target_pairs={{0,24},{8,16},{16,8},{24,0},{1,25},{9,17},{17,9},{25,1},{2,26},{10... | collective-permute-start | bytes 786440 | tf_op jit(solution)/shard_map/ppermute | solution.py:238
  7.8 20.6 %collective-permute-start.6 = (s32[1,17]{1,0:T(1,128)S(1)}, s32[1,17]{1,0:T(1,128)}, u32[]{:S(2)}, u32[]{:S(2)}) collective-permute-start(s32[1,17]{1,0:T(1,128)S(1)} %add_bitcast_fusion), channel_id=1, source_target_pairs={{0,1},{1,0},{2,3},{3,2},{4,5},{5,4},{6,7},{7,6},{8,9},{9,8},{10,11... | collective-permute-start | bytes 212 | tf_op jit(solution)/shard_map/ppermute | solution.py:238
  29.6 3.8 collective-permute-start.7
  34.6 4.8 %collective-permute-start.8 = (s32[4,17]{1,0:T(4,128)}, s32[4,17]{1,0:T(4,128)}, u32[]{:S(2)}, u32[]{:S(2)}) collective-permute-start(s32[4,17]{1,0:T(4,128)} %pad_add_fusion.1), channel_id=1, source_target_pairs={{0,4},{1,5},{2,6},{3,7},{4,0},{5,1},{6,2},{7,3},{8,12},{9,13},{10,... | collective-permute-start | bytes 824 | tf_op jit(solution)/shard_map/ppermute | solution.py:238
  191.5 33.0 %copy-start.3 = (bf16[3,768,768]{2,1,0:T(8,128)(2,1)}, bf16[3,768,768]{2,1,0:T(8,128)(2,1)S(1)}, u32[]{:S(2)}) copy-start(bf16[3,768,768]{2,1,0:T(8,128)(2,1)S(1)} %convolution_convert_fusion.4) | copy-start | bytes 10616836
  203.8 25.4 %copy-start.9 = (bf16[512,768]{1,0:T(8,128)(2,1)}, bf16[512,768]{1,0:T(8,128)(2,1)S(1)}, u32[]{:S(2)}) copy-start(bf16[512,768]{1,0:T(8,128)(2,1)S(1)} %convolution_convert_fusion.7) | copy-start | bytes 2359300
  220.1 69.3 %collective-permute-start.34 = (bf16[2,2,2,2,96,768]{5,4,3,2,1,0:T(8,128)(2,1)}, bf16[2,2,2,2,96,768]{5,4,3,2,1,0:T(8,128)(2,1)}, u32[]{:S(2)}, u32[]{:S(2)}) collective-permute-start(bf16[2,2,2,2,96,768]{5,4,3,2,1,0:T(8,128)(2,1)} %dynamic-slice_bitcast_fusion), channel_id=1, source_target_pairs={{0,8},{8,0},{16,24},{24,16},{1,9},{9,1},{17,25},{25,17},{2,10},{10... | collective-permute-start | bytes 7077896 | tf_op jit(solution)/shard_map/ppermute | solution.py:238
  221.8 73.5 %collective-permute-start.29 = (bf16[2,2,2,2,96,768]{5,4,3,2,1,0:T(8,128)(2,1)}, bf16[2,2,2,2,96,768]{5,4,3,2,1,0:T(8,128)(2,1)}, u32[]{:S(2)}, u32[]{:S(2)}) collective-permute-start(bf16[2,2,2,2,96,768]{5,4,3,2,1,0:T(8,128)(2,1)} %dynamic-slice_bitcast_fusion.1), channel_id=1, source_target_pairs={{0,8},{8,0},{16,24},{24,16},{1,9},{9,1},{17,25},{25,17},{2,10},{10... | collective-permute-start | bytes 7077896 | tf_op jit(solution)/shard_map/ppermute | solution.py:238
  223.1 22.4 %collective-permute-start.24 = (bf16[2,2,2,2,24,768]{5,4,3,2,1,0:T(8,128)(2,1)}, bf16[2,2,2,2,24,768]{5,4,3,2,1,0:T(8,128)(2,1)}, u32[]{:S(2)}, u32[]{:S(2)}) collective-permute-start(bf16[2,2,2,2,24,768]{5,4,3,2,1,0:T(8,128)(2,1)} %dynamic-slice_bitcast_fusion.3), channel_id=1, source_target_pairs={{0,8},{8,0},{16,24},{24,16},{1,9},{9,1},{17,25},{25,17},{2,10},{10... | collective-permute-start | bytes 1769480 | tf_op jit(solution)/shard_map/ppermute | solution.py:238
  224.0 9.7 %collective-permute-start.3 = (bf16[128,1024]{1,0:T(8,128)(2,1)}, bf16[128,1024]{1,0:T(8,128)(2,1)}, u32[]{:S(2)}, u32[]{:S(2)}) collective-permute-start(bf16[128,1024]{1,0:T(8,128)(2,1)} %get-tuple-element.76), channel_id=1, source_target_pairs={{0,8},{8,0},{16,24},{24,16},{1,9},{9,1},{17,25},{25,17},{2,10},{10... | collective-permute-start | bytes 786440 | tf_op jit(solution)/shard_map/ppermute | solution.py:238
  225.8 9.9 %collective-permute-start.4 = (bf16[128,1024]{1,0:T(8,128)(2,1)}, bf16[128,1024]{1,0:T(8,128)(2,1)}, u32[]{:S(2)}, u32[]{:S(2)}) collective-permute-start(bf16[128,1024]{1,0:T(8,128)(2,1)} %get-tuple-element.75), channel_id=1, source_target_pairs={{0,16},{8,24},{16,0},{24,8},{1,17},{9,25},{17,1},{25,9},{2,18},{10... | collective-permute-start | bytes 786440 | tf_op jit(solution)/shard_map/ppermute | solution.py:238
  233.8 3.5 collective-permute-start.9
  235.7 8.3 %collective-permute-start.5 = (bf16[128,1024]{1,0:T(8,128)(2,1)S(1)}, bf16[128,1024]{1,0:T(8,128)(2,1)S(1)}, u32[]{:S(2)}, u32[]{:S(2)}) collective-permute-start(bf16[128,1024]{1,0:T(8,128)(2,1)S(1)} %get-tuple-element.74), channel_id=1, source_target_pairs={{0,24},{8,16},{16,8},{24,0},{1,25},{9,17},{17,9},{25,1},{2,26},{10... | collective-permute-start | bytes 786440 | tf_op jit(solution)/shard_map/ppermute | solution.py:238
  237.3 56.4 %collective-permute-start.19 = (bf16[2,2,2,2,72,768]{5,4,3,2,1,0:T(8,128)(2,1)}, bf16[2,2,2,2,72,768]{5,4,3,2,1,0:T(8,128)(2,1)}, u32[]{:S(2)}, u32[]{:S(2)}) collective-permute-start(bf16[2,2,2,2,72,768]{5,4,3,2,1,0:T(8,128)(2,1)} %dynamic-slice_bitcast_fusion.2), channel_id=1, source_target_pairs={{0,8},{8,0},{16,24},{24,16},{1,9},{9,1},{17,25},{25,17},{2,10},{10... | collective-permute-start | bytes 5308424 | tf_op jit(solution)/shard_map/ppermute | solution.py:238
  244.1 7.8 %collective-permute-start.10 = (bf16[8,16,768]{2,1,0:T(8,128)(2,1)S(1)}, bf16[8,16,768]{2,1,0:T(8,128)(2,1)S(1)}, u32[]{:S(2)}, u32[]{:S(2)}) collective-permute-start(bf16[8,16,768]{2,1,0:T(8,128)(2,1)S(1)} %fusion.32), channel_id=1, source_target_pairs={{0,16},{8,24},{16,0},{24,8},{1,17},{9,25},{17,1},{25,9},{2,18},{10... | collective-permute-start | bytes 589832 | tf_op jit(solution)/shard_map/ppermute | solution.py:238
  247.8 38.5 %collective-permute-start.25 = (bf16[2,2,2,24,768]{4,3,2,1,0:T(8,128)(2,1)}, bf16[2,2,2,24,768]{4,3,2,1,0:T(8,128)(2,1)}, u32[]{:S(2)}, u32[]{:S(2)}) collective-permute-start(bf16[2,2,2,24,768]{4,3,2,1,0:T(8,128)(2,1)} %fusion.29), channel_id=1, source_target_pairs={{0,16},{8,24},{16,0},{24,8},{1,17},{9,25},{17,1},{25,9},{2,18},{10... | collective-permute-start | bytes 884744 | tf_op jit(solution)/shard_map/ppermute | solution.py:238
  253.0 27.2 %copy-start.14 = (f32[64,128]{1,0:T(8,128)S(1)}, f32[64,128]{1,0:T(8,128)}, u32[]{:S(2)}) copy-start(f32[64,128]{1,0:T(8,128)} %copy-done.13) | copy-start | bytes 98308
  253.1 27.2 %copy-start.15 = (f32[64,128]{1,0:T(8,128)S(1)}, f32[64,128]{1,0:T(8,128)}, u32[]{:S(2)}) copy-start(f32[64,128]{1,0:T(8,128)} %fusion.123) | copy-start | bytes 98308
  253.1 28.1 %copy-start.12 = (bf16[128,128]{1,0:T(8,128)(2,1)S(1)}, bf16[128,128]{1,0:T(8,128)(2,1)}, u32[]{:S(2)}) copy-start(bf16[128,128]{1,0:T(8,128)(2,1)} %param.22) | copy-start | bytes 98308
  253.2 28.2 %copy-start.19 = (s32[8]{0:T(128)S(1)}, s32[8]{0:T(128)}, u32[]{:S(2)}) copy-start(s32[8]{0:T(128)} %slice_reduce_fusion.1) | copy-start | bytes 100
  253.2 29.0 %copy-start.21 = (s32[64]{0:T(128)S(1)}, s32[64]{0:T(128)}, u32[]{:S(2)}) copy-start(s32[64]{0:T(128)} %copy-done.20) | copy-start | bytes 772
  253.2 42.0 %slice-start.4 = ((s8[4718592]{0:T(1024)(128)(4,1)}), s8[524288]{0:T(1024)(128)(4,1)S(1)}, s32[]{:S(2)}) async-start(s8[4718592]{0:T(1024)(128)(4,1)} %bitcast.427), calls=%async_computation.4 | async-start | bytes 1048576
  256.1 1.2 collective-permute-start.11
  257.4 3.8 collective-permute-start.12
  261.2 3.8 collective-permute-start.13
  265.0 3.9 collective-permute-start.14
  268.9 4.6 %collective-permute-start.16 = (bf16[4,1,8,1536]{3,2,0,1:T(8,128)(2,1)S(1)}, bf16[4,1,8,1536]{3,2,0,1:T(8,128)(2,1)S(1)}, u32[]{:S(2)}, u32[]{:S(2)}) collective-permute-start(bf16[4,1,8,1536]{3,2,0,1:T(8,128)(2,1)S(1)} %get-tuple-element.86), channel_id=1, source_target_pairs={{0,1},{1,0},{2,3},{3,2},{4,5},{5,4},{6,7},{7,6},{8,9},{9,8},{10,11... | collective-permute-start | bytes 294920 | tf_op jit(solution)/shard_map/ppermute | solution.py:238
  273.6 5.4 %collective-permute-start.15 = (f32[4,3328]{1,0:T(4,128)S(1)}, f32[4,3328]{1,0:T(4,128)S(1)}, u32[]{:S(2)}, u32[]{:S(2)}) collective-permute-start(f32[4,3328]{1,0:T(4,128)S(1)} %pad_maximum_fusion.4), channel_id=1, source_target_pairs={{0,4},{1,5},{2,6},{3,7},{4,0},{5,1},{6,2},{7,3},{8,12},{9,13},{10,... | collective-permute-start | bytes 159752 | tf_op jit(solution)/shard_map/ppermute | solution.py:238
  279.0 4.7 %collective-permute-start.17 = (bf16[2,2,8,1536]{3,2,0,1:T(8,128)(2,1)S(1)}, bf16[2,2,8,1536]{3,2,0,1:T(8,128)(2,1)S(1)}, u32[]{:S(2)}, u32[]{:S(2)}) collective-permute-start(bf16[2,2,8,1536]{3,2,0,1:T(8,128)(2,1)S(1)} %get-tuple-element.84), channel_id=1, source_target_pairs={{0,2},{1,3},{2,0},{3,1},{4,6},{5,7},{6,4},{7,5},{8,10},{9,11},{10,... | collective-permute-start | bytes 294920 | tf_op jit(solution)/shard_map/ppermute | solution.py:238
  283.8 5.6 %collective-permute-start.18 = (bf16[1,4,8,1536]{3,2,1,0:T(8,128)(2,1)S(1)}, bf16[1,4,8,1536]{3,2,1,0:T(8,128)(2,1)S(1)}, u32[]{:S(2)}, u32[]{:S(2)}) collective-permute-start(bf16[1,4,8,1536]{3,2,1,0:T(8,128)(2,1)S(1)} %get-tuple-element.82), channel_id=1, source_target_pairs={{0,4},{1,5},{2,6},{3,7},{4,0},{5,1},{6,2},{7,3},{8,12},{9,13},{10,... | collective-permute-start | bytes 294920 | tf_op jit(solution)/shard_map/ppermute | solution.py:238
  287.5 51.1 %collective-permute-start.26 = (bf16[2,2,24,768]{3,2,1,0:T(8,128)(2,1)S(1)}, bf16[2,2,24,768]{3,2,1,0:T(8,128)(2,1)S(1)}, u32[]{:S(2)}, u32[]{:S(2)}) collective-permute-start(bf16[2,2,24,768]{3,2,1,0:T(8,128)(2,1)S(1)} %fusion.40), channel_id=1, source_target_pairs={{0,4},{1,5},{2,6},{3,7},{4,0},{5,1},{6,2},{7,3},{8,12},{9,13},{10,... | collective-permute-start | bytes 442376 | tf_op jit(solution)/shard_map/ppermute | solution.py:238
  291.4 44.3 %collective-permute-start.35 = (bf16[2,2,2,96,768]{4,3,2,1,0:T(8,128)(2,1)S(1)}, bf16[2,2,2,96,768]{4,3,2,1,0:T(8,128)(2,1)S(1)}, u32[]{:S(2)}, u32[]{:S(2)}) collective-permute-start(bf16[2,2,2,96,768]{4,3,2,1,0:T(8,128)(2,1)S(1)} %fusion.12), channel_id=1, source_target_pairs={{0,16},{8,24},{16,0},{24,8},{1,17},{9,25},{17,1},{25,9},{2,18},{10... | collective-permute-start | bytes 3538952 | tf_op jit(solution)/shard_map/ppermute | solution.py:238
  295.1 36.6 %collective-permute-start.20 = (bf16[2,2,2,72,768]{4,3,2,1,0:T(8,128)(2,1)S(1)}, bf16[2,2,2,72,768]{4,3,2,1,0:T(8,128)(2,1)S(1)}, u32[]{:S(2)}, u32[]{:S(2)}) collective-permute-start(bf16[2,2,2,72,768]{4,3,2,1,0:T(8,128)(2,1)S(1)} %fusion.14), channel_id=1, source_target_pairs={{0,16},{8,24},{16,0},{24,8},{1,17},{9,25},{17,1},{25,9},{2,18},{10... | collective-permute-start | bytes 2654216 | tf_op jit(solution)/shard_map/ppermute | solution.py:238
  296.8 44.6 %collective-permute-start.30 = (bf16[2,2,2,96,768]{4,3,2,1,0:T(8,128)(2,1)S(1)}, bf16[2,2,2,96,768]{4,3,2,1,0:T(8,128)(2,1)S(1)}, u32[]{:S(2)}, u32[]{:S(2)}) collective-permute-start(bf16[2,2,2,96,768]{4,3,2,1,0:T(8,128)(2,1)S(1)} %fusion.13), channel_id=1, source_target_pairs={{0,2},{1,3},{2,0},{3,1},{4,6},{5,7},{6,4},{7,5},{8,10},{9,11},{10,... | collective-permute-start | bytes 3538952 | tf_op jit(solution)/shard_map/ppermute | solution.py:238
  332.9 27.8 %collective-permute-start.21 = (bf16[2,2,72,768]{3,2,1,0:T(8,128)(2,1)S(1)}, bf16[2,2,72,768]{3,2,1,0:T(8,128)(2,1)S(1)}, u32[]{:S(2)}, u32[]{:S(2)}) collective-permute-start(bf16[2,2,72,768]{3,2,1,0:T(8,128)(2,1)S(1)} %fusion.21), channel_id=1, source_target_pairs={{0,4},{1,5},{2,6},{3,7},{4,0},{5,1},{6,2},{7,3},{8,12},{9,13},{10,... | collective-permute-start | bytes 1327112 | tf_op jit(solution)/shard_map/ppermute | solution.py:238
  337.1 36.2 %collective-permute-start.36 = (bf16[2,2,96,768]{3,2,1,0:T(8,128)(2,1)S(1)}, bf16[2,2,96,768]{3,2,1,0:T(8,128)(2,1)S(1)}, u32[]{:S(2)}, u32[]{:S(2)}) collective-permute-start(bf16[2,2,96,768]{3,2,1,0:T(8,128)(2,1)S(1)} %fusion.16), channel_id=1, source_target_pairs={{0,4},{1,5},{2,6},{3,7},{4,0},{5,1},{6,2},{7,3},{8,12},{9,13},{10,... | collective-permute-start | bytes 1769480 | tf_op jit(solution)/shard_map/ppermute | solution.py:238
  339.6 12.5 %collective-permute-start.27 = (bf16[2,24,768]{2,1,0:T(8,128)(2,1)S(1)}, bf16[2,24,768]{2,1,0:T(8,128)(2,1)S(1)}, u32[]{:S(2)}, u32[]{:S(2)}) collective-permute-start(bf16[2,24,768]{2,1,0:T(8,128)(2,1)S(1)} %fusion.46), channel_id=1, source_target_pairs={{0,2},{1,3},{2,0},{3,1},{4,6},{5,7},{6,4},{7,5},{8,10},{9,11},{10,... | collective-permute-start | bytes 221192 | tf_op jit(solution)/shard_map/ppermute | solution.py:238
  342.7 36.4 %collective-permute-start.31 = (bf16[2,2,96,768]{3,2,1,0:T(8,128)(2,1)S(1)}, bf16[2,2,96,768]{3,2,1,0:T(8,128)(2,1)S(1)}, u32[]{:S(2)}, u32[]{:S(2)}) collective-permute-start(bf16[2,2,96,768]{3,2,1,0:T(8,128)(2,1)S(1)} %fusion.17), channel_id=1, source_target_pairs={{0,1},{1,0},{2,3},{3,2},{4,5},{5,4},{6,7},{7,6},{8,9},{9,8},{10,11... | collective-permute-start | bytes 1769480 | tf_op jit(solution)/shard_map/ppermute | solution.py:238
  353.0 21.6 %collective-permute-start.28 = (bf16[24,768]{1,0:T(8,128)(2,1)S(1)}, bf16[24,768]{1,0:T(8,128)(2,1)S(1)}, u32[]{:S(2)}, u32[]{:S(2)}) collective-permute-start(bf16[24,768]{1,0:T(8,128)(2,1)S(1)} %fusion.50), channel_id=1, source_target_pairs={{0,1},{1,0},{2,3},{3,2},{4,5},{5,4},{6,7},{7,6},{8,9},{9,8},{10,11... | collective-permute-start | bytes 110600 | tf_op jit(solution)/shard_map/ppermute | solution.py:238
  361.7 16.3 %collective-permute-start.22 = (bf16[2,72,768]{2,1,0:T(8,128)(2,1)S(1)}, bf16[2,72,768]{2,1,0:T(8,128)(2,1)S(1)}, u32[]{:S(2)}, u32[]{:S(2)}) collective-permute-start(bf16[2,72,768]{2,1,0:T(8,128)(2,1)S(1)} %fusion.31), channel_id=1, source_target_pairs={{0,2},{1,3},{2,0},{3,1},{4,6},{5,7},{6,4},{7,5},{8,10},{9,11},{10,... | collective-permute-start | bytes 663560 | tf_op jit(solution)/shard_map/ppermute | solution.py:238
  374.5 9.7 %collective-permute-start.37 = (bf16[2,96,768]{2,1,0:T(8,128)(2,1)S(1)}, bf16[2,96,768]{2,1,0:T(8,128)(2,1)S(1)}, u32[]{:S(2)}, u32[]{:S(2)}) collective-permute-start(bf16[2,96,768]{2,1,0:T(8,128)(2,1)S(1)} %fusion.27), channel_id=1, source_target_pairs={{0,2},{1,3},{2,0},{3,1},{4,6},{5,7},{6,4},{7,5},{8,10},{9,11},{10,... | collective-permute-start | bytes 884744 | tf_op jit(solution)/shard_map/ppermute | solution.py:238
  379.0 6.4 %collective-permute-start.23 = (bf16[72,768]{1,0:T(8,128)(2,1)S(1)}, bf16[72,768]{1,0:T(8,128)(2,1)S(1)}, u32[]{:S(2)}, u32[]{:S(2)}) collective-permute-start(bf16[72,768]{1,0:T(8,128)(2,1)S(1)} %fusion.41), channel_id=1, source_target_pairs={{0,1},{1,0},{2,3},{3,2},{4,5},{5,4},{6,7},{7,6},{8,9},{9,8},{10,11... | collective-permute-start | bytes 331784 | tf_op jit(solution)/shard_map/ppermute | solution.py:238
  380.2 8.9 %collective-permute-start.32 = (bf16[2,96,768]{2,1,0:T(8,128)(2,1)S(1)}, bf16[2,96,768]{2,1,0:T(8,128)(2,1)S(1)}, u32[]{:S(2)}, u32[]{:S(2)}) collective-permute-start(bf16[2,96,768]{2,1,0:T(8,128)(2,1)S(1)} %fusion.28), channel_id=1, source_target_pairs={{0,16},{8,24},{16,0},{24,8},{1,17},{9,25},{17,1},{25,9},{2,18},{10... | collective-permute-start | bytes 884744 | tf_op jit(solution)/shard_map/ppermute | solution.py:238
  385.4 5.7 %collective-permute-start.38 = (bf16[96,768]{1,0:T(8,128)(2,1)S(1)}, bf16[96,768]{1,0:T(8,128)(2,1)S(1)}, u32[]{:S(2)}, u32[]{:S(2)}) collective-permute-start(bf16[96,768]{1,0:T(8,128)(2,1)S(1)} %fusion.35), channel_id=1, source_target_pairs={{0,1},{1,0},{2,3},{3,2},{4,5},{5,4},{6,7},{7,6},{8,9},{9,8},{10,11... | collective-permute-start | bytes 442376 | tf_op jit(solution)/shard_map/ppermute | solution.py:238
  390.2 8.9 %collective-permute-start.33 = (bf16[96,768]{1,0:T(8,128)(2,1)S(1)}, bf16[96,768]{1,0:T(8,128)(2,1)S(1)}, u32[]{:S(2)}, u32[]{:S(2)}) collective-permute-start(bf16[96,768]{1,0:T(8,128)(2,1)S(1)} %fusion.37), channel_id=1, source_target_pairs={{0,4},{1,5},{2,6},{3,7},{4,0},{5,1},{6,2},{7,3},{8,12},{9,13},{10,... | collective-permute-start | bytes 442376 | tf_op jit(solution)/shard_map/ppermute | solution.py:238
  (24 other events, 188.9 us)
